TPU v7x, 128 devices: a whole 4x4x4 slice. The times are simulated.
128 devices in a mesh: dp: 8 (over x, core), tensor: 16 (over y, z).
Axes of the slice: x: 4, y: 4, z: 4, core: 2. Of those that a mesh axis runs over, the one named last changes fastest.
Arguments:
- tokens: bfloat16 [1536, 6144], P('dp', 'tensor'), may hold values from -6 to 6
- cotangent: bfloat16 [1536, 6144], P('dp', 'tensor'), may hold values from -6 to 6
- w1_blocks: bfloat16 [192, 15, 128, 128], P('tensor', None, 'dp'), may hold values from -0.125 to 0.125
- w1_rows: int32 [192, 15], replicated, may hold values from 0 to 47, all different within a row
- w1_scale: float32 [192, 15], replicated, may hold values from 0.5 to 2
- w2_blocks: bfloat16 [288, 15, 128, 128], P('tensor', None, 'dp'), may hold values from -0.0625 to 0.0625
- w2_cols: int32 [288, 15], replicated, may hold values from 0 to 47, all different within a row
- w2_scale: float32 [288, 15], replicated, may hold values from 0.5 to 2
- owner: int32 [192], replicated, may hold values from 0 to 15, as said below
Outputs:
- mixed: bfloat16 [1536, 6144], P('dp', 'tensor')
- input_grad: bfloat16 [1536, 6144], P('dp', 'tensor')
- grad_w1: bfloat16 [192, 15, 128, 128], P('tensor', None, 'dp')
- grad_w2: bfloat16 [288, 15, 128, 128], P('tensor', None, 'dp')
Inputs may be any that keep to these rules, and one draw needn't show every extreme that they name: `owner`: hidden block g is computed from first-projection rows held on tensor index g // 12. Every tensor index owns at most 18 hidden blocks, and at most 2 of the hidden blocks of one tensor index are owned by one index; some index owns exactly 18 and some pair reaches 2 in every draw. `w1_rows`: each row names 15 different feature blocks. `w2_cols`: each row names 15 different feature blocks.
All inputs are finite; a program needn't handle non-finite values.
Results may differ from a plain program's by a relative error of at most 0.02.
Values may be sent and summed in bfloat16 or wider, within the bound.
A program may use at most 192 MiB of HBM per device.

v0:
```python
import jax
import jax.numpy as jnp
from jax import lax
from jax.sharding import PartitionSpec as P

GELU_C = 0.7978845608028654
GELU_A = 0.044715


def gelu_value(h):
    inner = GELU_C * (h + GELU_A * h * h * h)
    return 0.5 * h * (1.0 + jnp.tanh(inner))


def gelu_slope(h):
    inner = GELU_C * (h + GELU_A * h * h * h)
    tanh_val = jnp.tanh(inner)
    return 0.5 * (1.0 + tanh_val) + 0.5 * h * (1.0 - tanh_val * tanh_val) * GELU_C * (
        1.0 + 3.0 * GELU_A * h * h
    )


def route_tables(owner, per_dev):
    count = owner.shape[0]
    index = jnp.arange(count, dtype=jnp.int32)
    source = index // per_dev
    earlier = index[None, :] < index[:, None]
    same_dest = owner[None, :] == owner[:, None]
    same_src = source[None, :] == source[:, None]
    slot = jnp.sum((earlier & same_dest).astype(jnp.int32), axis=1)
    pair = jnp.sum((earlier & same_dest & same_src).astype(jnp.int32), axis=1)
    return (source, slot, pair)


def dequantize(values, scale):
    return (values.astype(jnp.float32) * scale[:, :, None, None]).astype(jnp.bfloat16)


def first_match(match):
    index = jnp.arange(match.shape[1], dtype=jnp.int32)
    found = jnp.sum(jnp.where(match, index[None, :], 0), axis=1)
    return (found, jnp.any(match, axis=1))


def pick(array, index, live, axis):
    taken = jnp.take(array, index, axis=axis)
    shape = [1] * taken.ndim
    shape[axis] = live.shape[0]
    return jnp.where(live.reshape(shape), taken, jnp.zeros_like(taken))


def place_blocks(terms, targets, col_blocks):
    rows_dev = terms.shape[0]
    block = terms.shape[-1]
    flat = terms.reshape(rows_dev, -1, block)
    empty = jnp.zeros((rows_dev, col_blocks, block), jnp.float32)
    return empty.at[:, targets.reshape(-1)].add(flat).reshape(rows_dev, col_blocks * block)


def local(tokens, cotangent, w1_blocks, w1_rows, w1_scale, w2_blocks, w2_cols, w2_scale, owner):
    groups = lax.axis_size("tensor")
    rank = lax.axis_index("tensor")
    per_dev = w1_blocks.shape[0]
    capacity = w2_blocks.shape[0]
    block = w1_blocks.shape[3]
    pair_most = (capacity + groups - 1) // groups
    source, slot, pair = route_tables(owner, per_dev)
    lanes = jnp.arange(groups * pair_most, dtype=jnp.int32)
    lane_peer = lanes // pair_most
    lane_pair = lanes % pair_most
    mine = rank * per_dev + jnp.arange(per_dev, dtype=jnp.int32)
    own_match = (
        (owner[None, :] == rank)
        & (source[None, :] == lane_peer[:, None])
        & (pair[None, :] == lane_pair[:, None])
    )
    own_block, own_live = first_match(own_match)
    own_slot = slot[own_block]
    home_match = (owner[mine][None, :] == lane_peer[:, None]) & (
        pair[mine][None, :] == lane_pair[:, None]
    )
    home_local, home_live = first_match(home_match)
    home_recv = owner[mine] * pair_most + pair[mine]
    slots_all = jnp.arange(capacity, dtype=jnp.int32)
    slot_match = (owner[None, :] == rank) & (slot[None, :] == slots_all[:, None])
    slot_block, slot_live = first_match(slot_match)
    slot_recv = source[slot_block] * pair_most + pair[slot_block]
    full_x, full_dy = (
        lax.all_gather(tokens, "tensor", axis=1, tiled=True),
        lax.all_gather(cotangent, "tensor", axis=1, tiled=True),
    )
    rows_dev = full_x.shape[0]
    width = full_x.shape[1]
    col_blocks = width // block
    x_cube = full_x.reshape(rows_dev, col_blocks, block)
    dy_cube = full_dy.reshape(rows_dev, col_blocks, block)
    my_rows = w1_rows[mine]
    my_scale_one = w1_scale[mine]
    where_two = rank * capacity + slots_all
    cols_here = w2_cols[where_two]
    scale_here = w2_scale[where_two]
    w1_full, w2_full = (
        lax.all_gather(w1_blocks, "dp", axis=2, tiled=True),
        lax.all_gather(w2_blocks, "dp", axis=2, tiled=True),
    )
    weff_one = dequantize(w1_full, my_scale_one)
    weff_two = dequantize(w2_full, scale_here)
    x_sel = x_cube[:, my_rows]
    pre = jnp.einsum("tcbi,cbio->tco", x_sel, weff_one, preferred_element_type=jnp.float32)
    act = gelu_value(pre).astype(jnp.bfloat16)
    arrived = lax.all_to_all(
        pick(act, home_local, home_live, 1), "tensor", split_axis=1, concat_axis=1, tiled=True
    )
    act_here = pick(arrived, slot_recv, slot_live, 1)
    z_two = jnp.einsum("tsi,sbio->tsbo", act_here, weff_two, preferred_element_type=jnp.float32)
    y_part = place_blocks(z_two, cols_here, col_blocks)
    mixed = lax.psum_scatter(y_part.astype(jnp.bfloat16), "tensor", scatter_dimension=1, tiled=True)
    dy_sel = dy_cube[:, cols_here]
    dact_here = jnp.einsum(
        "tsbo,sbio->tsi", dy_sel, weff_two, preferred_element_type=jnp.float32
    ).astype(jnp.bfloat16)
    gw_two = jnp.einsum("tsi,tsbo->sbio", act_here, dy_sel, preferred_element_type=jnp.float32)
    returned = lax.all_to_all(
        pick(dact_here, own_slot, own_live, 1), "tensor", split_axis=1, concat_axis=1, tiled=True
    )
    d_act = jnp.take(returned, home_recv, axis=1)
    d_pre = (d_act.astype(jnp.float32) * gelu_slope(pre)).astype(jnp.bfloat16)
    gw_one = jnp.einsum("tcbi,tco->cbio", x_sel, d_pre, preferred_element_type=jnp.float32)
    z_one = jnp.einsum("tco,cbio->tcbi", d_pre, weff_one, preferred_element_type=jnp.float32)
    dx_part = place_blocks(z_one, my_rows, col_blocks)
    input_grad = lax.psum_scatter(
        dx_part.astype(jnp.bfloat16), "tensor", scatter_dimension=1, tiled=True
    )
    sum_one, sum_two = (
        lax.psum_scatter(gw_one.astype(jnp.bfloat16), "dp", scatter_dimension=2, tiled=True).astype(
            jnp.float32
        ),
        lax.psum_scatter(gw_two.astype(jnp.bfloat16), "dp", scatter_dimension=2, tiled=True).astype(
            jnp.float32
        ),
    )
    grad_one = (sum_one * my_scale_one[:, :, None, None]).astype(jnp.bfloat16)
    grad_here = (sum_two * scale_here[:, :, None, None]).astype(jnp.bfloat16)
    return (mixed, input_grad, grad_one, grad_here)


def solution(mesh):
    in_specs = (
        P("dp", "tensor"),
        P("dp", "tensor"),
        P("tensor", None, "dp", None),
        P(),
        P(),
        P("tensor", None, "dp", None),
        P(),
        P(),
        P(),
    )
    out_specs = (
        P("dp", "tensor"),
        P("dp", "tensor"),
        P("tensor", None, "dp", None),
        P("tensor", None, "dp", None),
    )
    return jax.shard_map(local, mesh=mesh, in_specs=in_specs, out_specs=out_specs, check_vma=False)
```

profile of v0, /device:TPU:0, one launch (start us, length us, event | category | flops | bytes accessed | tf_op | source)
XLA Modules:
  0.0 578.0 jit_solution(4449532396060622869)
XLA Ops:
  7.2 0.7 all-gather.9.cloned.1.call-update
  8.0 0.7 all-gather.7.cloned.1.call-update
  8.7 0.7 all-gather.5.cloned.1.call-update
  10.3 0.7 gather_fusion.4
  11.0 0.7 gather_fusion.5
  12.2 0.7 gather_fusion.3
  12.9 0.7 gather_fusion.2
  14.5 0.7 gather_fusion.11
  17.4 44.2 %all-gather.9.cloned.1.call-done = bf16[192,6144]{1,0:T(8,128)(2,1)} async-done(((bf16[192,384]{1,0:T(8,128)(2,1)}), bf16[192,6144]{1,0:T(8,128)(2,1)}) %all-gather.9.cloned.1.call-update) | async-done | bytes 2359312 | tf_op jit(solution)/shard_map/all_gather | solution.py:89
  61.6 2.3 copy_bitcast_fusion.1
  64.0 9.7 %gather_fusion.8 = bf16[180,192,128]{2,1,0:T(8,128)(2,1)} fusion(bf16[192,48,128]{2,0,1:T(8,128)(2,1)S(1)} %copy_bitcast_fusion.1, s32[1024]{0:T(1024)S(1)} %pad_clamp_fusion.6), kind=kCustom, calls=%fused_computation.8 | custom fusion | bytes 17695440 | tf_op jit(solution)/shard_map/gather | solution.py:108
  73.6 32.2 %all-gather.7.cloned.1.call-done = bf16[12,15,128,128]{3,2,1,0:T(8,128)(2,1)} async-done(((bf16[12,15,16,128]{3,2,1,0:T(8,128)(2,1)}), bf16[12,15,128,128]{3,2,1,0:T(8,128)(2,1)}) %all-gather.7.cloned.1.call-update) | async-done | bytes 5898256 | tf_op jit(solution)/shard_map/all_gather | solution.py:103
  105.8 8.9 %multiply_convert_fusion.14 = (bf16[192,12,128]{2,0,1:T(8,128)(2,1)S(1)}, f32[192,12,128]{2,0,1:T(8,128)}) fusion(bf16[192,12,15,128]{3,0,2,1:T(8,128)(2,1)} %bitcast.123, bf16[12,15,128,128]{3,2,1,0:T(8,128)(2,1)} %all-gather.7.cloned.1.call-done, f32[12,15]{1,0:T(8,128)S(1)} %gather_fusion.6), kind=kOutput, calls=%fused_computation.43 | convolution fusion | flops 1143963648 | bytes 16515792 | tf_op jit(solution)/shard_map/tcbi,cbio->tco/dot_general | solution.py:109
  114.7 0.8 gather_fusion.9
  115.5 1.5 select_bitcast_fusion.1
  117.1 7.0 %all-to-all-start = ((bf16[192,32,128]{2,0,1:T(8,128)(2,1)}), bf16[192,32,128]{2,0,1:T(8,128)(2,1)S(1)}, u32[]{:S(2)}, u32[]{:S(2)}) async-start(bf16[192,32,128]{2,0,1:T(8,128)(2,1)} %select_bitcast_fusion.1), calls=%async_computation | async-start | bytes 3145728 | tf_op jit(solution)/shard_map/all_to_all | solution.py:111
  125.0 23.6 %all-to-all-done = bf16[192,32,128]{2,0,1:T(8,128)(2,1)S(1)} async-done(((bf16[192,32,128]{2,0,1:T(8,128)(2,1)}), bf16[192,32,128]{2,0,1:T(8,128)(2,1)S(1)}, u32[]{:S(2)}, u32[]{:S(2)}) %all-to-all-start) | async-done | bytes 1572896 | tf_op jit(solution)/shard_map/all_to_all | solution.py:111
  148.6 0.7 gather_fusion.10
  149.3 15.1 %all-gather.5.cloned.1.call-done = bf16[18,15,128,128]{3,2,1,0:T(8,128)(2,1)} async-done(((bf16[18,15,16,128]{3,2,1,0:T(8,128)(2,1)}), bf16[18,15,128,128]{3,2,1,0:T(8,128)(2,1)}) %all-gather.5.cloned.1.call-update) | async-done | bytes 8847376 | tf_op jit(solution)/shard_map/all_gather | solution.py:104
  164.4 16.1 %fusion.1 = f32[18,15,128,192]{2,3,1,0:T(8,128)} fusion(bf16[18,15,128,128]{3,2,1,0:T(8,128)(2,1)} %all-gather.5.cloned.1.call-done, f32[18,15]{1,0:T(8,128)S(1)} %gather_fusion.1, bf16[18,192,128]{2,1,0:T(8,128)(2,1)S(1)} %gather_fusion.10, pred[18]{0:T(512)(128)(4,1)S(1)} %fusion.19, pred[18]{0:T(512)(128)(4,1)S(1)} %compare_and_fusion.5), kind=kOutput, calls=%fused_computation.21 | convolution fusion | flops 1712848896 | bytes 36275292 | tf_op jit(solution)/shard_map/tsi,sbio->tsbo/dot_general | solution.py:115
  180.5 2.7 broadcast.407.clone
  183.3 68.7 %scatter_fusion = f32[192,48,128]{2,0,1:T(8,128)} fusion(f32[192,48,128]{2,0,1:T(8,128)} %broadcast.407.clone, s32[270]{0:T(512)S(1)} %fusion.22, f32[270,192,128]{2,1,0:T(8,128)} %bitcast.117), kind=kCustom, calls=%fused_computation.15 | custom fusion | flops 6635520 | bytes 79627320 | tf_op jit(solution)/shard_map/scatter-add | solution.py:57
  252.0 2.7 convert_element_type.73
  254.7 2.8 copy.64
  257.6 2.3 copy_bitcast_fusion
  259.9 12.0 %gather_fusion.12 = bf16[270,192,128]{2,1,0:T(8,128)(2,1)} fusion(bf16[192,48,128]{2,0,1:T(8,128)(2,1)S(1)} %copy_bitcast_fusion, s32[1024]{0:T(1024)S(1)} %pad_clamp_fusion.2), kind=kCustom, calls=%fused_computation.12 | custom fusion | bytes 26543160 | tf_op jit(solution)/shard_map/gather | solution.py:118
  271.9 12.1 %fusion.5 = bf16[192,18,128]{2,0,1:T(8,128)(2,1)} fusion(bf16[192,18,15,128]{3,0,2,1:T(8,128)(2,1)} %bitcast.118, bf16[18,15,128,128]{3,2,1,0:T(8,128)(2,1)} %all-gather.5.cloned.1.call-done, f32[18,15]{1,0:T(8,128)S(1)} %gather_fusion.1), kind=kOutput, calls=%fused_computation.35 | convolution fusion | flops 1712406528 | bytes 23004216 | tf_op jit(solution)/shard_map/tsbo,sbio->tsi/dot_general | solution.py:119
  283.9 2.0 gather_fusion.13
  286.0 1.4 select_bitcast_fusion
  287.4 7.2 %all-to-all-start.1 = ((bf16[192,32,128]{2,0,1:T(8,128)(2,1)}), bf16[192,32,128]{2,0,1:T(8,128)(2,1)S(1)}, u32[]{:S(2)}, u32[]{:S(2)}) async-start(bf16[192,32,128]{2,0,1:T(8,128)(2,1)} %select_bitcast_fusion), calls=%async_computation.1 | async-start | bytes 3145728 | tf_op jit(solution)/shard_map/all_to_all | solution.py:123
  295.0 26.7 %all-to-all-done.1 = bf16[192,32,128]{2,0,1:T(8,128)(2,1)S(1)} async-done(((bf16[192,32,128]{2,0,1:T(8,128)(2,1)}), bf16[192,32,128]{2,0,1:T(8,128)(2,1)S(1)}, u32[]{:S(2)}, u32[]{:S(2)}) %all-to-all-start.1) | async-done | bytes 1572896 | tf_op jit(solution)/shard_map/all_to_all | solution.py:123
  322.3 11.9 %fusion.2 = f32[12,15,128,192]{2,3,1,0:T(8,128)} fusion(bf16[12,15,128,128]{3,2,1,0:T(8,128)(2,1)} %all-gather.7.cloned.1.call-done, f32[12,15]{1,0:T(8,128)S(1)} %gather_fusion.6, f32[192,12,128]{2,0,1:T(8,128)} %get-tuple-element.27, bf16[12,192,128]{2,1,0:T(8,128)(2,1)S(1)} %gather_fusion.14, pred[12]{0:T(512)(128)(4,1)S(1)} %compare_and_fusion.3), kind=kOutput, calls=%fused_computation.22 | convolution fusion | flops 1147502592 | bytes 25363164 | tf_op jit(solution)/shard_map/tco,cbio->tcbi/dot_general | solution.py:129
  334.3 2.7 broadcast.407.clone.1
  337.0 48.0 %scatter_fusion.1 = f32[192,48,128]{2,0,1:T(8,128)} fusion(f32[192,48,128]{2,0,1:T(8,128)} %broadcast.407.clone.1, s32[180]{0:T(256)S(1)} %bitcast.127, f32[180,192,128]{2,1,0:T(8,128)} %bitcast.120), kind=kCustom, calls=%fused_computation.16 | custom fusion | flops 4423680 | bytes 53084880 | tf_op jit(solution)/shard_map/scatter-add | solution.py:57
  385.0 2.7 convert_element_type.79
  387.7 2.8 copy.65
  390.6 1.0 copy-done.2
  392.0 10.4 %convolution_convert_fusion = bf16[12,15,128,128]{3,2,1,0:T(8,128)(2,1)} fusion(bf16[192,12,15,128]{3,0,2,1:T(8,128)(2,1)} %bitcast.124, f32[192,12,128]{2,0,1:T(8,128)S(1)} %copy-done.3, bf16[12,192,128]{2,1,0:T(8,128)(2,1)S(1)} %copy-done.2, pred[12]{0:T(512)(128)(4,1)S(1)} %compare_and_fusion.3), kind=kOutput, calls=%fused_computation.24 | convolution fusion | flops 1141604352 | bytes 16515084 | tf_op jit(solution)/shard_map/tcbi,tco->cbio/dot_general | solution.py:128
  402.7 10.9 %convert_bitcast_fusion = bf16[18,15,128,128]{2,3,1,0:T(8,128)(2,1)} fusion(bf16[192,18,15,128]{3,0,2,1:T(8,128)(2,1)} %bitcast.119, bf16[18,192,128]{2,1,0:T(8,128)(2,1)S(1)} %gather_fusion.10, pred[18]{0:T(512)(128)(4,1)S(1)} %fusion.19, pred[18]{0:T(512)(128)(4,1)S(1)} %compare_and_fusion.5), kind=kOutput, calls=%fused_computation.19 | convolution fusion | flops 1704001536 | bytes 23003172 | tf_op jit(solution)/shard_map/tsi,tsbo->sbio/dot_general | solution.py:122
  413.5 13.3 %copy.54 = bf16[18,15,128,128]{3,1,0,2:T(8,128)(2,1)} copy(bf16[18,15,128,128]{2,3,1,0:T(8,128)(2,1)} %convert_bitcast_fusion) | data formatting | bytes 17694720 | tf_op jit(solution)/shard_map/convert_element_type | solution.py:138
  426.9 1.7 copy.61
  428.6 36.8 %reduce-scatter.15.cloned.1.call-done = bf16[384,192]{1,0:T(8,128)(2,1)} async-done(((bf16[6144,192]{1,0:T(8,128)(2,1)}), bf16[384,192]{1,0:T(8,128)(2,1)}) %reduce-scatter.15.cloned.1.call-update) | async-done | bytes 147472
  465.4 1.7 copy.63
  467.1 41.4 %reduce-scatter.9.cloned.1.call-done = bf16[12,15,16,128]{3,2,1,0:T(8,128)(2,1)} async-done(((bf16[12,15,128,128]{3,2,1,0:T(8,128)(2,1)}), bf16[12,15,16,128]{3,2,1,0:T(8,128)(2,1)}) %reduce-scatter.9.cloned.1.call-update) | async-done | bytes 737296 | tf_op jit(solution)/shard_map/reduce_scatter | solution.py:135
  508.5 2.2 multiply_convert_fusion.9
  510.7 57.2 %reduce-scatter.11.cloned.1.call-done = bf16[18,15,16,128]{3,1,0,2:T(8,128)(2,1)} async-done(((bf16[18,15,128,128]{3,1,0,2:T(8,128)(2,1)}), bf16[18,15,16,128]{3,1,0,2:T(8,128)(2,1)}) %reduce-scatter.11.cloned.1.call-update) | async-done | bytes 1105936 | tf_op jit(solution)/shard_map/reduce_scatter | solution.py:138
  568.0 1.6 multiply_convert_fusion.6
  569.5 1.4 copy.55
  (79 shorter events, 7.2 us)
Async XLA Ops:
  7.2 2.9 copy-start
  7.2 54.5 %all-gather.9.cloned.1.call-start = ((), (), s32[]{:S(2)}) async-start(), calls=%async_computation.8 | async-start | bytes 2506752 | tf_op jit(solution)/shard_map/all_gather | solution.py:89
  7.9 97.9 %all-gather.7.cloned.1.call-start = ((), (), s32[]{:S(2)}) async-start(), calls=%async_computation.7 | async-start | bytes 6635520 | tf_op jit(solution)/shard_map/all_gather | solution.py:103
  8.7 5.0 copy-start.4
  8.7 155.8 %all-gather.5.cloned.1.call-start = ((), (), s32[]{:S(2)}) async-start(), calls=%async_computation.6 | async-start | bytes 9953280 | tf_op jit(solution)/shard_map/all_gather | solution.py:104
  9.4 5.8 %copy-start.6 = (s32[192,15]{0,1:T(8,128)S(1)}, s32[192,15]{0,1:T(8,128)}, u32[]{:S(2)}) copy-start(s32[192,15]{0,1:T(8,128)} %param.12) | copy-start | bytes 34564
  9.4 248.1 %all-gather.11.cloned.1.call-start = ((), (), s32[]{:S(2)}) async-start(), calls=%async_computation.9 | async-start | bytes 2506752 | tf_op jit(solution)/shard_map/all_gather | solution.py:90
  10.3 5.7 copy-start.7
  11.0 5.8 copy-start.5
  117.1 31.5 %all-to-all-start = ((bf16[192,32,128]{2,0,1:T(8,128)(2,1)}), bf16[192,32,128]{2,0,1:T(8,128)(2,1)S(1)}, u32[]{:S(2)}, u32[]{:S(2)}) async-start(bf16[192,32,128]{2,0,1:T(8,128)(2,1)} %select_bitcast_fusion.1), calls=%async_computation | async-start | bytes 3145728 | tf_op jit(solution)/shard_map/all_to_all | solution.py:111
  124.0 302.8 %reduce-scatter.13.cloned.1.call-start = ((), (), s32[]{:S(2)}) async-start(), calls=%async_computation.12 | async-start | bytes 3342336
  287.4 34.3 %all-to-all-start.1 = ((bf16[192,32,128]{2,0,1:T(8,128)(2,1)}), bf16[192,32,128]{2,0,1:T(8,128)(2,1)S(1)}, u32[]{:S(2)}, u32[]{:S(2)}) async-start(bf16[192,32,128]{2,0,1:T(8,128)(2,1)} %select_bitcast_fusion), calls=%async_computation.1 | async-start | bytes 3145728 | tf_op jit(solution)/shard_map/all_to_all | solution.py:123
  294.6 170.8 %reduce-scatter.15.cloned.1.call-start = ((), (), s32[]{:S(2)}) async-start(), calls=%async_computation.13 | async-start | bytes 3342336
  322.3 12.0 %copy-start.1 = (bf16[12,192,128]{2,1,0:T(8,128)(2,1)}, bf16[12,192,128]{2,1,0:T(8,128)(2,1)S(1)}, u32[]{:S(2)}) copy-start(bf16[12,192,128]{2,1,0:T(8,128)(2,1)S(1)} %gather_fusion.14) | copy-start | bytes 1769476
  390.5 1.1 copy-start.2
  390.5 1.5 copy-start.3
  390.6 117.9 %reduce-scatter.9.cloned.1.call-start = ((), (), s32[]{:S(2)}) async-start(), calls=%async_computation.10 | async-start | bytes 6635520 | tf_op jit(solution)/shard_map/reduce_scatter | solution.py:135
  402.4 165.6 %reduce-scatter.11.cloned.1.call-start = ((), (), s32[]{:S(2)}) async-start(), calls=%async_computation.11 | async-start | bytes 10616832 | tf_op jit(solution)/shard_map/reduce_scatter | solution.py:138
Sparse Core Ops, SparseCore 0:
  10.1 51.4 all-gather.8
  63.3 42.4 all-gather.6
  107.5 56.8 all-gather.4
  166.4 49.9 all-gather.10
  257.7 89.8 reduce-scatter.12
  390.7 74.6 reduce-scatter.14
  467.8 40.6 reduce-scatter.8
  511.0 56.8 reduce-scatter.10
where the time goes:
time: 586 us; the launch traced here: 578 us
  waiting for transfers between devices  280 us (48%)
  other arithmetic  130 us (22%)
  matrix products  70.2 us (12%)
  local copies, waits for them, and re-layouts  67.6 us (12%)
  starting transfers between devices  15.4 us (3%)
  between operations  14.8 us (3%)
    scatter-add x2, other arithmetic, place_blocks(): empty.at[:, targets.reshape(-1)].add(flat)  117 us
    reduce_scatter x1, waiting for transfers between devices, local(): lax.psum_scatter(gw_two.astype(jnp.bfloat16), 'dp', scatter_dimension=2,...  57.2 us
    all_gather x1, waiting for transfers between devices, local(): lax.all_gather(tokens, 'tensor', axis=1, tiled=True)  44.2 us
    reduce_scatter x1, waiting for transfers between devices, local(): lax.psum_scatter(gw_one.astype(jnp.bfloat16), 'dp', scatter_dimension=2,...  41.4 us
    unnamed x10, waiting for transfers between devices  39.5 us
    all_gather x1, waiting for transfers between devices, local(): lax.all_gather(w1_blocks, 'dp', axis=2, tiled=True)  32.2 us
    all_to_all x1, waiting for transfers between devices, local(): lax.all_to_all(pick(dact_here, own_slot, own_live, 1), 'tensor', split_ax...  26.7 us
    all_to_all x1, waiting for transfers between devices, local(): lax.all_to_all(pick(act, home_local, home_live, 1), 'tensor', split_axis=...  23.6 us
  transfers between devices with their start and end apart: 10, of which 8 were waited for; matrix products, arithmetic and copies ran while one was open for 46% of the time, Pallas kernels for 0%

commit v1 on v0

v1 whole, which is shorter than its diff:
```python
import jax
import jax.numpy as jnp
from jax import lax
from jax.experimental import pallas as pl
from jax.experimental.pallas import tpu as pltpu
from jax.sharding import PartitionSpec as P

GELU_C = 0.7978845608028654
GELU_A = 0.044715
MESH = pl.DeviceIdType.MESH
BF = jnp.bfloat16
F32 = jnp.float32
NB = 12
NK = 15
CAP = 18
HALF = NB // 2


def where_am_i():
    p = lax.axis_index("dp")
    t = lax.axis_index("tensor")
    return p, t, p // 2, p % 2, t // 4, t % 4


def enter(p, t, x, c, y, z):
    barrier = pltpu.get_barrier_semaphore()
    for d in range(1, 16):
        peer = ((y + d // 4) % 4) * 4 + (z + d % 4) % 4
        pl.semaphore_signal(barrier, inc=1, device_id=(p, peer), device_id_type=MESH)
    for q in (2 * ((x + 1) % 4) + c, 2 * ((x + 3) % 4) + c, 2 * x + 1 - c):
        pl.semaphore_signal(barrier, inc=1, device_id=(q, t), device_id_type=MESH)
    return barrier


def gather_kernel(
    tok_ref,
    cot_ref,
    w1_ref,
    w2_ref,
    s1_ref,
    s2_ref,
    own_slot_ref,
    home_lane_ref,
    xall,
    dyall,
    w1all,
    w2all,
    tok3,
    cot3,
    e1s,
    e2s,
    lanes,
    rbuf,
    a_send,
    a_recv,
    w_send,
    w_recv,
    x_send,
    x_recv,
    l_sem,
):
    p, t, x, c, y, z = where_am_i()
    barrier = enter(p, t, x, c, y, z)
    rp, lp, op, sp = 2 * ((x + 1) % 4) + c, 2 * ((x + 3) % 4) + c, 2 * ((x + 2) % 4) + c, 2 * x + 1 - c

    def copy_lane(i, _):
        s = own_slot_ref[i]
        lanes[i] = w2_ref[s]
        return 0

    lax.fori_loop(0, 32, copy_lane, 0)

    def scale_one(g, _):
        for k in range(NK):
            e1s[g, k] = (w1_ref[g, k].astype(F32) * s1_ref[g, k]).astype(BF)
        return 0

    lax.fori_loop(0, NB, scale_one, 0)
    for b in range(3):
        tok3[b] = tok_ref[:, b * 128 : (b + 1) * 128]
        cot3[b] = cot_ref[:, b * 128 : (b + 1) * 128]

    def lane_copy(d):
        peer = ((y + d // 4) % 4) * 4 + (z + d % 4) % 4
        return pltpu.make_async_remote_copy(
            lanes.at[pl.ds(2 * peer, 2)],
            rbuf.at[pl.ds(2 * t, 2)],
            a_send.at[d],
            a_recv.at[d],
            device_id=(p, peer),
            device_id_type=MESH,
        )

    def weight_copy(w, i):
        e, a = ((e1s, w1all), (e2s, w2all))[w]
        first, second = pl.ds(0, HALF), pl.ds(HALF, HALF)
        src, dst, dev = (
            (e.at[first], a.at[p, first], rp),
            (e.at[second], a.at[p, second], rp),
            (e.at[second], a.at[p, second], lp),
            (e.at[first], a.at[p, first], lp),
            (e, a.at[p], sp),
            (a.at[lp, first], a.at[lp, first], rp),
            (a.at[rp, second], a.at[rp, second], lp),
            (a.at[lp], a.at[lp], sp),
            (a.at[rp], a.at[rp], sp),
            (a.at[op], a.at[op], sp),
        )[i]
        return pltpu.make_async_remote_copy(
            src, dst, w_send.at[w, i], w_recv.at[w, i], device_id=(dev, t), device_id_type=MESH
        )

    def feature_copy(w, first, second):
        own, full = ((tok3, xall), (cot3, dyall))[w]
        if second == 0:
            src = own
            holder = t
            ay, az = (first, 0) if w == 0 else (0, first)
        else:
            by, bz = (first, 0) if w == 0 else (0, first)
            holder = ((y + 4 - by) % 4) * 4 + (z + 4 - bz) % 4
            src = own if first == 0 else full.at[holder]
            ay, az = (0, second) if w == 0 else (second, 0)
        peer = ((y + ay) % 4) * 4 + (z + az) % 4
        return pltpu.make_async_remote_copy(
            src,
            full.at[holder],
            x_send.at[w, first, second],
            x_recv.at[w, first, second],
            device_id=(p, peer),
            device_id_type=MESH,
        )

    pl.semaphore_wait(barrier, 18)
    for d in range(1, 16):
        lane_copy(d).start()
    for i in range(5):
        weight_copy(0, i).start()
    local = [
        pltpu.make_async_copy(tok3, xall.at[t], l_sem.at[0]),
        pltpu.make_async_copy(cot3, dyall.at[t], l_sem.at[1]),
        pltpu.make_async_copy(e1s, w1all.at[p], l_sem.at[2]),
    ]
    for cp in local:
        cp.start()
    for first in range(1, 4):
        for w in range(2):
            feature_copy(w, first, 0).start()

    def weights_on(w):
        weight_copy(w, 0).wait_recv()
        weight_copy(w, 5).start()
        weight_copy(w, 2).wait_recv()
        weight_copy(w, 6).start()
        weight_copy(w, 1).wait_recv()
        weight_copy(w, 7).start()
        weight_copy(w, 3).wait_recv()
        weight_copy(w, 8).start()

    for second in range(1, 4):
        for w in range(2):
            feature_copy(w, 0, second).start()
    weights_on(0)
    for d in range(1, 16):
        lane_copy(d).wait_recv()
    rbuf[pl.ds(2 * t, 2)] = lanes[pl.ds(2 * t, 2)]

    def scale_two(g, _):
        i = home_lane_ref[g]
        for k in range(NK):
            e2s[g, k] = (rbuf[i, k].astype(F32) * s2_ref[g, k]).astype(BF)
        return 0

    lax.fori_loop(0, NB, scale_two, 0)
    for i in range(5):
        weight_copy(1, i).start()
    keep = pltpu.make_async_copy(e2s, w2all.at[p], l_sem.at[3])
    keep.start()
    local.append(keep)
    for first in range(1, 4):
        for w in range(2):
            feature_copy(w, first, 0).wait_recv()
            for second in range(1, 4):
                feature_copy(w, first, second).start()
    weight_copy(0, 5).wait_recv()
    weight_copy(0, 6).wait_recv()
    weight_copy(0, 9).start()
    weights_on(1)
    weight_copy(1, 5).wait_recv()
    weight_copy(1, 6).wait_recv()
    weight_copy(1, 9).start()
    for first in range(4):
        for second in range(1, 4):
            for w in range(2):
                feature_copy(w, first, second).wait_recv()
    for w in range(2):
        for i in (4, 7, 8, 9):
            weight_copy(w, i).wait_recv()
    for cp in local:
        cp.wait()
    for d in range(1, 16):
        lane_copy(d).wait_send()
    for w in range(2):
        for i in range(10):
            weight_copy(w, i).wait_send()
        for first in range(4):
            for second in range(4):
                if first or second:
                    feature_copy(w, first, second).wait_send()


def compute_kernel(
    rows, cols, x_ref, dy_ref, w1_ref, w2_ref, m_ref, d_ref, g1_ref, g2_ref, acc_m, acc_d, xt
):
    g = pl.program_id(0)

    @pl.when(g == 0)
    def _():
        acc_m[...] = jnp.zeros_like(acc_m)
        acc_d[...] = jnp.zeros_like(acc_d)

        def flip(j, _):
            xt[j] = x_ref[j].T
            return 0

        lax.fori_loop(0, 48, flip, 0)

    nt = (((1,), (1,)), ((), ()))
    r = [rows[g, k] for k in range(NK)]
    q = [cols[g, k] for k in range(NK)]
    w1c = jnp.concatenate([w1_ref[:, 0, k].reshape(128, 128) for k in range(NK)], axis=0)
    w2c = jnp.concatenate([w2_ref[:, 0, k].reshape(128, 128) for k in range(NK)], axis=1)
    xs = jnp.concatenate([x_ref[r[k]] for k in range(NK)], axis=1)
    dys = jnp.concatenate([dy_ref[q[k]] for k in range(NK)], axis=1)
    pre = jnp.dot(xs, w1c, preferred_element_type=F32)
    dact = lax.dot_general(dys, w2c, nt, preferred_element_type=F32).astype(BF)
    th = jnp.tanh(GELU_C * (pre + GELU_A * pre * pre * pre))
    act = (0.5 * pre * (1.0 + th)).astype(BF)
    slope = 0.5 * (1.0 + th) + 0.5 * pre * (1.0 - th * th) * GELU_C * (
        1.0 + 3.0 * GELU_A * pre * pre
    )
    dpre = (dact.astype(F32) * slope).astype(BF)
    mix = jnp.dot(act, w2c, preferred_element_type=F32)
    for k in range(NK):
        acc_m[q[k]] += mix[:, k * 128 : (k + 1) * 128]
    dx = lax.dot_general(dpre, w1c, nt, preferred_element_type=F32)
    for k in range(NK):
        acc_d[r[k]] += dx[:, k * 128 : (k + 1) * 128]
    gw2 = jnp.dot(act.T, dys, preferred_element_type=F32).astype(BF)
    for k in range(NK):
        g2_ref[:, 0, k] = gw2[:, k * 128 : (k + 1) * 128].reshape(8, 16, 128)
        g1_ref[:, 0, k] = (
            jnp.dot(xt[r[k]], dpre, preferred_element_type=F32).astype(BF).reshape(8, 16, 128)
        )

    @pl.when(g == pl.num_programs(0) - 1)
    def _():
        def out(j, _):
            m_ref[j] = acc_m[j].astype(BF)
            d_ref[j] = acc_d[j].astype(BF)
            return 0

        lax.fori_loop(0, 48, out, 0)


def reduce_kernel(
    m_ref,
    d_ref,
    g1_ref,
    g2_ref,
    s1_ref,
    s2_ref,
    home_local_ref,
    slot_lane_ref,
    slot_live_ref,
    mixed,
    dxo,
    o1,
    o2,
    own,
    sib,
    fwd,
    fin,
    red2,
    lanes,
    rbuf,
    f_own,
    f_buf,
    f_sum,
    f_fin,
    w_send,
    w_recv,
    f_send,
    f_recv,
    a_send,
    a_recv,
    l_sem,
):
    p, t, x, c, y, z = where_am_i()
    barrier = enter(p, t, x, c, y, z)
    xr, xl, xo = (x + 1) % 4, (x + 3) % 4, (x + 2) % 4
    rp, lp, sp = 2 * xr + c, 2 * xl + c, 2 * x + 1 - c
    grads = (g2_ref, g1_ref)
    feats = (m_ref, d_ref)
    first, second = pl.ds(0, HALF), pl.ds(HALF, HALF)

    def grad_copy(w, i):
        src, dst, dev = (
            (own.at[w, xo, first], fwd.at[w, 0], rp),
            (own.at[w, xo, second], fwd.at[w, 1], lp),
            (own.at[w, xr, second], fin.at[w, 0, second], rp),
            (own.at[w, xl, first], fin.at[w, 1, first], lp),
            (own.at[w, xr, first], fin.at[w, 0, first], rp),
            (own.at[w, xl, second], fin.at[w, 1, second], lp),
            (grads[w].at[:, 1 - c], sib.at[w], sp),
        )[i]
        return pltpu.make_async_remote_copy(
            src, dst, w_send.at[w, i], w_recv.at[w, i], device_id=(dev, t), device_id_type=MESH
        )

    def feat_copy(w, step, d):
        along_y = (w == 0) == (step == 0)
        peer_y, peer_z = ((y + d) % 4, z) if along_y else (y, (z + d) % 4)
        if step == 0:
            src = feats[w].at[peer_y] if along_y else feats[w].at[:, peer_z]
            dst = f_buf.at[w, d - 1]
        else:
            src = f_sum.at[w, peer_y if along_y else peer_z]
            dst = f_fin.at[w, d - 1]
        return pltpu.make_async_remote_copy(
            src,
            dst,
            f_send.at[w, step, d],
            f_recv.at[w, step, d],
            device_id=(p, peer_y * 4 + peer_z),
            device_id_type=MESH,
        )

    def lane_copy(d):
        peer = ((y + d // 4) % 4) * 4 + (z + d % 4) % 4
        return pltpu.make_async_remote_copy(
            lanes.at[pl.ds(2 * peer, 2)],
            rbuf.at[pl.ds(2 * t, 2)],
            a_send.at[d],
            a_recv.at[d],
            device_id=(p, peer),
            device_id_type=MESH,
        )

    local = [pltpu.make_async_copy(grads[w].at[:, c], own.at[w], l_sem.at[w]) for w in range(2)]
    local.append(pltpu.make_async_copy(m_ref.at[y], f_own.at[0], l_sem.at[2]))
    local.append(pltpu.make_async_copy(d_ref.at[:, z], f_own.at[1], l_sem.at[3]))
    for cp in local:
        cp.start()
    pl.semaphore_wait(barrier, 18)
    grad_copy(0, 6).start()
    for d in range(1, 4):
        for w in range(2):
            feat_copy(w, 0, d).start()
    grad_copy(1, 6).start()

    def pair_sum(w, chunk, lo, n):
        def body(g, _):
            own[w, chunk, g] = (own[w, chunk, g].astype(F32) + sib[w, chunk, g].astype(F32)).astype(
                BF
            )
            return 0

        lax.fori_loop(lo, lo + n, body, 0)

    def pair_stage(w):
        local[w].wait()
        grad_copy(w, 6).wait_recv()
        pair_sum(w, xo, 0, NB)
        grad_copy(w, 0).start()
        grad_copy(w, 1).start()
        pair_sum(w, xr, HALF, HALF)
        grad_copy(w, 2).start()
        pair_sum(w, xl, 0, HALF)
        grad_copy(w, 3).start()
        pair_sum(w, xr, 0, HALF)
        pair_sum(w, xl, HALF, HALF)
        pair_sum(w, x, 0, NB)

    def pass_stage(w):
        grad_copy(w, 0).wait_recv()

        def right(g, _):
            own[w, xr, g] = (own[w, xr, g].astype(F32) + fwd[w, 0, g].astype(F32)).astype(BF)
            return 0

        lax.fori_loop(0, HALF, right, 0)
        grad_copy(w, 4).start()
        grad_copy(w, 1).wait_recv()

        def left(g, _):
            own[w, xl, g + HALF] = (
                own[w, xl, g + HALF].astype(F32) + fwd[w, 1, g].astype(F32)
            ).astype(BF)
            return 0

        lax.fori_loop(0, HALF, left, 0)
        grad_copy(w, 5).start()

    def last_stage(w, out, scale):
        for i in (2, 3, 4, 5):
            grad_copy(w, i).wait_recv()

        def body(g, _):
            for k in range(NK):
                total = own[w, x, g, k].astype(F32) + fin[w, 0, g, k].astype(F32)
                total = total + fin[w, 1, g, k].astype(F32)
                out[g, k] = (total * scale[g, k]).astype(BF)
            return 0

        lax.fori_loop(0, NB, body, 0)

    pair_stage(0)
    for w in range(2):
        local[2 + w].wait()
        for d in range(1, 4):
            feat_copy(w, 0, d).wait_recv()

        def add_four(i, _):
            a, b = i // 3, i % 3
            total = f_own[w, a, b].astype(F32)
            for d in range(3):
                total = total + f_buf[w, d, a, b].astype(F32)
            f_sum[w, a, b] = total.astype(BF)
            return 0

        lax.fori_loop(0, 12, add_four, 0)
        for d in range(1, 4):
            feat_copy(w, 1, d).start()
    pass_stage(0)
    pair_stage(1)
    for w, out in ((0, mixed), (1, dxo)):
        for d in range(1, 4):
            feat_copy(w, 1, d).wait_recv()
        here = z if w == 0 else y
        for b in range(3):
            total = f_sum[w, here, b].astype(F32)
            for d in range(3):
                total = total + f_fin[w, d, b].astype(F32)
            out[:, b * 128 : (b + 1) * 128] = total.astype(BF)
    last_stage(0, red2, s2_ref)

    def copy_lane(i, _):
        s = home_local_ref[i]
        lanes[i] = red2[s]
        return 0

    lax.fori_loop(0, 32, copy_lane, 0)
    for d in range(1, 16):
        lane_copy(d).start()
    rbuf[pl.ds(2 * t, 2)] = lanes[pl.ds(2 * t, 2)]
    pass_stage(1)
    for d in range(1, 16):
        lane_copy(d).wait_recv()

    def slot_out(s, _):
        i = slot_lane_ref[s]
        o2[s] = jnp.where(slot_live_ref[s] > 0, rbuf[i], jnp.zeros_like(rbuf[i]))
        return 0

    lax.fori_loop(0, CAP, slot_out, 0)
    last_stage(1, o1, s1_ref)
    for w in range(2):
        for i in range(7):
            grad_copy(w, i).wait_send()
        for step in range(2):
            for d in range(1, 4):
                feat_copy(w, step, d).wait_send()
    for d in range(1, 16):
        lane_copy(d).wait_send()


def route_tables(owner, rank):
    index = jnp.arange(192, dtype=jnp.int32)
    source = index // NB
    earlier = index[None, :] < index[:, None]
    same_dest = owner[None, :] == owner[:, None]
    same_src = source[None, :] == source[:, None]
    slot = jnp.sum((earlier & same_dest).astype(jnp.int32), axis=1)
    pair = jnp.sum((earlier & same_dest & same_src).astype(jnp.int32), axis=1)
    mine_first = rank * NB
    mine_owner = lax.dynamic_slice(owner, (mine_first,), (NB,))
    mine_pair = lax.dynamic_slice(pair, (mine_first,), (NB,))
    mine_slot = lax.dynamic_slice(slot, (mine_first,), (NB,))
    home_lane = mine_owner * 2 + mine_pair
    home_q = mine_owner * CAP + mine_slot
    lane = jnp.arange(32, dtype=jnp.int32)
    mine_lane = jnp.where(owner == rank, source * 2 + pair, -1)
    own_slot = jnp.sum(jnp.where(lane[:, None] == mine_lane[None, :], slot[None, :], 0), axis=1)
    home_local = jnp.sum(
        jnp.where(
            lane[:, None] == home_lane[None, :], jnp.arange(NB, dtype=jnp.int32)[None, :], 0
        ),
        axis=1,
    )
    mine_at = jnp.where(owner == rank, slot, -1)
    hit = jnp.arange(CAP, dtype=jnp.int32)[:, None] == mine_at[None, :]
    slot_lane = jnp.sum(jnp.where(hit, (source * 2 + pair)[None, :], 0), axis=1)
    slot_live = jnp.any(hit, axis=1).astype(jnp.int32)
    return home_lane, home_q, own_slot, home_local, slot_lane, slot_live


VM = pl.BlockSpec(memory_space=pltpu.VMEM)
SM = pl.BlockSpec(memory_space=pltpu.SMEM)
ANY = pl.BlockSpec(memory_space=pl.ANY)
SHARD = (NB, NK, 16, 128)
LANES = (32, NK, 16, 128)


def local(tokens, cotangent, w1_blocks, w1_rows, w1_scale, w2_blocks, w2_cols, w2_scale, owner):
    rank = lax.axis_index("tensor")
    home_lane, home_q, own_slot, home_local, slot_lane, slot_live = route_tables(owner, rank)
    rows = lax.dynamic_slice(w1_rows, (rank * NB, 0), (NB, NK))
    scale_one = lax.dynamic_slice(w1_scale, (rank * NB, 0), (NB, NK))
    cols = w2_cols[home_q]
    scale_two = w2_scale[home_q]
    dma = pltpu.SemaphoreType.DMA
    xall, dyall, w1all, w2all = pl.pallas_call(
        gather_kernel,
        out_shape=[
            jax.ShapeDtypeStruct((16, 3, 192, 128), BF),
            jax.ShapeDtypeStruct((16, 3, 192, 128), BF),
            jax.ShapeDtypeStruct((8,) + SHARD, BF),
            jax.ShapeDtypeStruct((8,) + SHARD, BF),
        ],
        in_specs=[VM, VM, VM, VM, SM, SM, SM, SM],
        out_specs=[ANY] * 4,
        scratch_shapes=[
            pltpu.VMEM((3, 192, 128), BF),
            pltpu.VMEM((3, 192, 128), BF),
            pltpu.VMEM(SHARD, BF),
            pltpu.VMEM(SHARD, BF),
            pltpu.VMEM(LANES, BF),
            pltpu.VMEM(LANES, BF),
            dma((16,)),
            dma((16,)),
            dma((2, 10)),
            dma((2, 10)),
            dma((2, 4, 4)),
            dma((2, 4, 4)),
            dma((4,)),
        ],
        compiler_params=pltpu.CompilerParams(
            collective_id=0, has_side_effects=True, vmem_limit_bytes=40 << 20
        ),
    )(tokens, cotangent, w1_blocks, w2_blocks, scale_one, scale_two, own_slot, home_lane)
    whole = pl.BlockSpec((48, 192, 128), lambda g, *_: (0, 0, 0))
    blocks = pl.BlockSpec((8, 1, NK, 16, 128), lambda g, *_: (0, g, 0, 0, 0))
    m_part, d_part, g1, g2 = pl.pallas_call(
        compute_kernel,
        grid_spec=pltpu.PrefetchScalarGridSpec(
            num_scalar_prefetch=2,
            grid=(NB,),
            in_specs=[whole, whole, blocks, blocks],
            out_specs=[whole, whole, blocks, blocks],
            scratch_shapes=[
                pltpu.VMEM((48, 192, 128), F32),
                pltpu.VMEM((48, 192, 128), F32),
                pltpu.VMEM((48, 128, 192), BF),
            ],
        ),
        out_shape=[
            jax.ShapeDtypeStruct((48, 192, 128), BF),
            jax.ShapeDtypeStruct((48, 192, 128), BF),
            jax.ShapeDtypeStruct((8,) + SHARD, BF),
            jax.ShapeDtypeStruct((8,) + SHARD, BF),
        ],
        compiler_params=pltpu.CompilerParams(
            dimension_semantics=("arbitrary",), vmem_limit_bytes=56 << 20
        ),
    )(rows, cols, xall.reshape(48, 192, 128), dyall.reshape(48, 192, 128), w1all, w2all)
    feat = (4, 4, 3, 192, 128)
    grad = (4, 2) + SHARD
    mixed, dx, o1, o2 = pl.pallas_call(
        reduce_kernel,
        out_shape=[
            jax.ShapeDtypeStruct((192, 384), BF),
            jax.ShapeDtypeStruct((192, 384), BF),
            jax.ShapeDtypeStruct(SHARD, BF),
            jax.ShapeDtypeStruct((CAP, NK, 16, 128), BF),
        ],
        in_specs=[ANY] * 4 + [SM] * 5,
        out_specs=[VM] * 4,
        scratch_shapes=[
            pltpu.VMEM((2, 4) + SHARD, BF),
            pltpu.VMEM((2, 4) + SHARD, BF),
            pltpu.VMEM((2, 2, HALF, NK, 16, 128), BF),
            pltpu.VMEM((2, 2) + SHARD, BF),
            pltpu.VMEM(SHARD, BF),
            pltpu.VMEM(LANES, BF),
            pltpu.VMEM(LANES, BF),
            pltpu.VMEM((2, 4, 3, 192, 128), BF),
            pltpu.VMEM((2, 3, 4, 3, 192, 128), BF),
            pltpu.VMEM((2, 4, 3, 192, 128), BF),
            pltpu.VMEM((2, 3, 3, 192, 128), BF),
            dma((2, 7)),
            dma((2, 7)),
            dma((2, 2, 4)),
            dma((2, 2, 4)),
            dma((16,)),
            dma((16,)),
            dma((4,)),
        ],
        compiler_params=pltpu.CompilerParams(
            collective_id=1, has_side_effects=True, vmem_limit_bytes=48 << 20
        ),
    )(
        m_part.reshape(feat),
        d_part.reshape(feat),
        g1.reshape(grad),
        g2.reshape(grad),
        scale_one,
        scale_two,
        home_local,
        slot_lane,
        slot_live,
    )
    return mixed, dx, o1, o2


def solution(mesh):
    in_specs = (
        P("dp", "tensor"),
        P("dp", "tensor"),
        P("tensor", None, "dp", None),
        P(),
        P(),
        P("tensor", None, "dp", None),
        P(),
        P(),
        P(),
    )
    out_specs = (
        P("dp", "tensor"),
        P("dp", "tensor"),
        P("tensor", None, "dp", None),
        P("tensor", None, "dp", None),
    )
    return jax.shard_map(local, mesh=mesh, in_specs=in_specs, out_specs=out_specs, check_vma=False)
```

time: 586 us -> 193 us (0.33); the launches traced: 578 us -> 192 us
  waiting for transfers between devices: 280 us -> 0 us
  Pallas kernels: 0 us -> 168 us
  other arithmetic: 130 us -> 2.9 us
  matrix products: 70.2 us -> 0 us
  local copies, waits for them, and re-layouts: 67.6 us -> 19.5 us
  starting transfers between devices: 15.4 us -> 0 us
  between operations: 14.8 us -> 0.75 us
    pallas_call x0 -> x3, Pallas kernels: none -> 168 us  [the longest x1 71.5 us: local(): pl.pallas_call(reduce_kernel, out_shape=[jax.ShapeDtypeStruct((192, 384),...]
    scatter-add x2 -> x0, other arithmetic: 117 us -> none  [place_blocks(): empty.at[:, targets.reshape(-1)].add(flat)]
    reduce_scatter x2 -> x0, waiting for transfers between devices: 98.6 us -> none  [the longest x1 57.2 us: local(): lax.psum_scatter(gw_two.astype(jnp.bfloat16), 'dp', scatter_dimension=2,...]
    all_gather x4 -> x0, waiting for transfers between devices: 91.5 us -> none  [the longest x1 44.2 us: local(): lax.all_gather(tokens, 'tensor', axis=1, tiled=True)]
    dot_general x6 -> x0, matrix products: 70.2 us -> none  [the longest x1 16.1 us: local(): jnp.einsum('tsi,sbio->tsbo', act_here, weff_two, preferred_element_type=j...]
    all_to_all x2 -> x0, waiting for transfers between devices: 50.3 us -> none  [the longest x1 26.7 us: local(): lax.all_to_all(pick(dact_here, own_slot, own_live, 1), 'tensor', split_ax...]
    unnamed x10 -> x0, waiting for transfers between devices: 39.5 us -> none
    gather x15 -> x2, local copies, waits for them, and re-layouts: 31.6 us -> 1.72 us  [the longest x1 1.15 us: local(): cols = w2_cols[home_q]]
  transfers between devices with their start and end apart: 10 -> 0, of which waited for: 8 -> 0; matrix products, arithmetic and copies ran while one was open for 46% -> 0% of each run, Pallas kernels for 0% -> 0%
where the time goes in v1:
time: 193 us; the launch traced here: 192 us
  Pallas kernels  168 us (87%)
  local copies, waits for them, and re-layouts  19.5 us (10%)
  other arithmetic  2.9 us (2%)
    pallas_call x1, Pallas kernels, local(): pl.pallas_call(reduce_kernel, out_shape=[jax.ShapeDtypeStruct((192, 384),...  71.5 us
    pallas_call x1, Pallas kernels, local(): pl.pallas_call(gather_kernel, out_shape=[jax.ShapeDtypeStruct((16, 3, 192...  68.3 us
    pallas_call x1, Pallas kernels, local(): pl.pallas_call(compute_kernel, grid_spec=pltpu.PrefetchScalarGridSpec(num...  28.5 us
    unnamed x26, local copies, waits for them, and re-layouts  17 us

profile of v1, /device:TPU:0, one launch (start us, length us, event | category | flops | bytes accessed | tf_op | source)
XLA Modules:
  0.0 191.5 jit_solution(8021396158034538098)
XLA Ops:
  0.6 0.0 copy-start
  0.7 1.0 convert_reduce_fusion
  1.7 0.8 dynamic-slice_add_fusion
  2.4 0.1 select_reduce_fusion.2.home_local_ref
  2.5 0.7 broadcast_select_fusion
  3.2 0.1 select_reduce_fusion.own_slot_ref
  3.3 0.1 select_reduce_fusion.1.slot_lane_ref
  3.4 0.1 fusion.1
  3.6 0.0 copy-done
  3.6 0.1 constant_dynamic-slice_fusion.1
  3.7 0.7 copy.21.rows
  4.4 0.8 constant_dynamic-slice_fusion
  5.2 0.1 copy.22.s1_ref
  5.2 0.8 copy.18
  6.1 1.2 gather_fusion
  7.3 0.8 copy.20
  8.1 0.6 gather_fusion.1
  8.7 0.0 copy-start.5
  8.7 1.2 copy-done.5
  9.9 0.0 copy-start.6
  9.9 1.1 copy-done.6
  11.0 0.0 copy-start.7
  11.0 0.9 copy-done.7
  11.9 0.0 copy-start.8
  11.9 0.9 copy-done.8
  12.8 68.3 %shard_map.120 = (bf16[16,3,192,128]{3,2,1,0:T(8,128)(2,1)S(1)}, bf16[16,3,192,128]{3,2,1,0:T(8,128)(2,1)S(1)}, bf16[8,12,15,16,128]{4,3,2,1,0:T(8,128)(2,1)S(1)}, bf16[8,12,15,16,128]{4,3,2,1,0:T(8,128)(2,1)}) custom-call(bf16[192,384]{1,0:T(8,128)(2,1)S(1)} %copy-done.7, bf16[192,384]{1,0:T(8,128)(2,1)S(1)} %copy-done.8, ...), custom_call_target="tpu_custom_call" | custom-call | tf_op jit(solution)/shard_map/pallas_call | solution.py:523
  81.2 0.0 copy-start.1
  81.2 2.6 %copy-done.1 = bf16[8,12,15,16,128]{4,3,2,1,0:T(8,128)(2,1)} copy-done((bf16[8,12,15,16,128]{4,3,2,1,0:T(8,128)(2,1)}, bf16[8,12,15,16,128]{4,3,2,1,0:T(8,128)(2,1)S(1)}, u32[]{:S(2)}) %copy-start.1) | copy-done | bytes 5898264
  83.7 0.0 copy-start.2
  83.7 1.5 copy-done.2
  85.2 0.0 copy-start.3
  85.2 1.4 copy-done.3
  86.7 28.5 %shard_map.121 = (bf16[48,192,128]{2,1,0:T(8,128)(2,1)}, bf16[48,192,128]{2,1,0:T(8,128)(2,1)}, bf16[8,12,15,16,128]{4,3,2,1,0:T(8,128)(2,1)}, bf16[8,12,15,16,128]{4,3,2,1,0:T(8,128)(2,1)}) custom-call(s32[12,15]{1,0:T(8,128)} %copy.21.rows, s32[12,15]{1,0:T(8,128)} %gather_fusion, bf16[48,192,128]{2,1,0:T(8,128)(2,1)} %bitcast.6, ...), custom_call_target="tpu_custom_call" | custom-call | tf_op jit(solution)/shard_map/pallas_call | solution.py:554
  115.2 0.0 copy-start.4
  115.2 1.7 copy-done.4
  116.8 71.5 %shard_map.122 = (bf16[192,384]{1,0:T(8,128)(2,1)S(1)}, bf16[192,384]{1,0:T(8,128)(2,1)S(1)}, bf16[12,15,16,128]{3,2,1,0:T(8,128)(2,1)S(1)}, bf16[18,15,16,128]{3,2,1,0:T(8,128)(2,1)S(1)}) custom-call(bf16[4,4,3,192,128]{4,3,2,1,0:T(8,128)(2,1)S(1)} %bitcast.8, bf16[4,4,3,192,128]{4,3,2,1,0:T(8,128)(2,1)} %bitcast.11, ...), custom_call_target="tpu_custom_call" | custom-call | tf_op jit(solution)/shard_map/pallas_call | solution.py:579
  188.3 0.7 copy.27
  189.0 0.7 copy.28
  189.6 0.9 copy.29
  190.5 1.0 copy.30
  (3 shorter events, 0.0 us)
Async XLA Ops:
  0.6 3.0 %copy-start = (s32[192,15]{0,1:T(8,128)S(1)}, s32[192,15]{0,1:T(8,128)}, u32[]{:S(2)}) copy-start(s32[192,15]{0,1:T(8,128)} %param.12) | copy-start | bytes 34564
  8.7 1.2 copy-start.5
  9.9 1.1 copy-start.6
  11.0 0.9 copy-start.7
  11.9 0.9 copy-start.8
  81.2 2.6 %copy-start.1 = (bf16[8,12,15,16,128]{4,3,2,1,0:T(8,128)(2,1)}, bf16[8,12,15,16,128]{4,3,2,1,0:T(8,128)(2,1)S(1)}, u32[]{:S(2)}) copy-start(bf16[8,12,15,16,128]{4,3,2,1,0:T(8,128)(2,1)S(1)} %get-tuple-element.14.w1_ref) | copy-start | bytes 17694724
  83.7 1.5 copy-start.2
  85.2 1.4 copy-start.3
  115.2 1.7 copy-start.4

commit v2 on v0

v2 whole, which is shorter than its diff:
```python
import jax
import jax.numpy as jnp
from jax import lax
from jax.experimental import pallas as pl
from jax.experimental.pallas import tpu as pltpu
from jax.sharding import PartitionSpec as P

GELU_C = 0.7978845608028654
GELU_A = 0.044715
MESH = pl.DeviceIdType.MESH
BF = jnp.bfloat16
F32 = jnp.float32
NB = 12
NK = 15
CAP = 18
HALF = NB // 2


def where_am_i():
    p = lax.axis_index("dp")
    t = lax.axis_index("tensor")
    return p, t, p // 2, p % 2, t // 4, t % 4


def enter(p, t, x, c, y, z):
    barrier = pltpu.get_barrier_semaphore()
    for d in range(1, 16):
        peer = ((y + d // 4) % 4) * 4 + (z + d % 4) % 4
        pl.semaphore_signal(barrier, inc=1, device_id=(p, peer), device_id_type=MESH)
    for q in (2 * ((x + 1) % 4) + c, 2 * ((x + 3) % 4) + c, 2 * x + 1 - c):
        pl.semaphore_signal(barrier, inc=1, device_id=(q, t), device_id_type=MESH)
    return barrier


def layer_kernel(
    tok_ref,
    cot_ref,
    w1_ref,
    w2_ref,
    s1_ref,
    s2_ref,
    rows,
    cols,
    kv1,
    kv2,
    own_slot_ref,
    home_lane_ref,
    home_local_ref,
    slot_lane_ref,
    slot_live_ref,
    mixed,
    dxo,
    o1,
    o2,
    w1in,
    w2in,
    xall,
    dyall,
    w1all,
    w2all,
    lanes,
    rbuf,
    rback,
    xt,
    slope,
    act_all,
    dpre_all,
    g1s,
    g2s,
    sib,
    fwd,
    fin,
    m_part,
    d_part,
    f_buf,
    f_fin,
    a_send,
    a_recv,
    b_send,
    b_recv,
    w_send,
    w_recv,
    x_send,
    x_recv,
    g_send,
    g_recv,
    f_send,
    f_recv,
    l_sem,
    free_sem,
):
    p, t, x, c, y, z = where_am_i()
    barrier = enter(p, t, x, c, y, z)
    xr, xl, xo = (x + 1) % 4, (x + 3) % 4, (x + 2) % 4
    rp, lp, op, sp = 2 * xr + c, 2 * xl + c, 2 * xo + c, 2 * x + 1 - c
    halves = (pl.ds(0, HALF), pl.ds(HALF, HALF))
    first, second = halves
    whole = pl.ds(0, NB)
    feats = (xall, dyall)
    weights = (w1all, w2all)
    grads = (g2s, g1s)
    parts = (m_part, d_part)
    nt = (((1,), (1,)), ((), ()))

    def lane_copy(back, d):
        peer = ((y + d // 4) % 4) * 4 + (z + d % 4) % 4
        return pltpu.make_async_remote_copy(
            lanes.at[pl.ds(2 * peer, 2)],
            (rback if back else rbuf).at[pl.ds(2 * t, 2)],
            (b_send if back else a_send).at[d],
            (b_recv if back else a_recv).at[d],
            device_id=(p, peer),
            device_id_type=MESH,
        )

    def weight_copy(w, i):
        who, part, dev = (
            (p, first, rp),
            (p, second, rp),
            (p, second, lp),
            (p, first, lp),
            (p, whole, sp),
            (lp, first, rp),
            (rp, second, lp),
            (lp, whole, sp),
            (rp, whole, sp),
            (op, whole, sp),
        )[i]
        ref = weights[w].at[who, part, pl.ds(0, NK)]
        return pltpu.make_async_remote_copy(
            ref, ref, w_send.at[w, i], w_recv.at[w, i], device_id=(dev, t), device_id_type=MESH
        )

    def feature_copy(w, one, two):
        if two == 0:
            holder = t
            ay, az = (one, 0) if w == 0 else (0, one)
        else:
            by, bz = (one, 0) if w == 0 else (0, one)
            holder = ((y + 4 - by) % 4) * 4 + (z + 4 - bz) % 4
            ay, az = (0, two) if w == 0 else (two, 0)
        peer = ((y + ay) % 4) * 4 + (z + az) % 4
        ref = feats[w].at[pl.ds(3 * holder, 3)]
        return pltpu.make_async_remote_copy(
            ref,
            ref,
            x_send.at[w, one, two],
            x_recv.at[w, one, two],
            device_id=(p, peer),
            device_id_type=MESH,
        )

    def grad_copy(w, i):
        own = grads[w]
        src, dst, dev = (
            (own.at[xo, c, first], fwd.at[w, 0], rp),
            (own.at[xo, c, second], fwd.at[w, 1], lp),
            (own.at[xr, c, second], fin.at[w, 0, second], rp),
            (own.at[xl, c, first], fin.at[w, 1, first], lp),
            (own.at[xr, c, first], fin.at[w, 0, first], rp),
            (own.at[xl, c, second], fin.at[w, 1, second], lp),
            (own.at[:, 1 - c, first], sib.at[:, first], sp),
            (own.at[:, 1 - c, second], sib.at[:, second], sp),
        )[i]
        return pltpu.make_async_remote_copy(
            src, dst, g_send.at[w, i], g_recv.at[w, i], device_id=(dev, t), device_id_type=MESH
        )

    def part_copy(w, step, d):
        along_y = (w == 0) == (step == 0)
        peer_y, peer_z = ((y + d) % 4, z) if along_y else (y, (z + d) % 4)
        if step == 0:
            src = parts[w].at[peer_y] if along_y else parts[w].at[:, peer_z]
            dst = f_buf.at[w, d - 1]
        else:
            src = parts[w].at[peer_y, peer_z]
            dst = f_fin.at[w, d - 1]
        return pltpu.make_async_remote_copy(
            src,
            dst,
            f_send.at[w, step, d],
            f_recv.at[w, step, d],
            device_id=(p, peer_y * 4 + peer_z),
            device_id_type=MESH,
        )

    loads = [
        pltpu.make_async_copy(w2_ref, w2in, l_sem.at[0]),
        pltpu.make_async_copy(w1_ref, w1in, l_sem.at[1]),
    ]
    for w, ref in enumerate((tok_ref, cot_ref)):
        for b in range(3):
            loads.append(
                pltpu.make_async_copy(
                    ref.at[:, pl.ds(b * 128, 128)],
                    feats[w].at[3 * t + b],
                    l_sem.at[2 + 3 * w + b],
                )
            )
    for cp in loads:
        cp.start()
    loads[0].wait()

    def lanes_out(i, _):
        s = own_slot_ref[i]
        lanes[i] = w2in[s]
        return 0

    lax.fori_loop(0, 32, lanes_out, 0)
    pl.semaphore_wait(barrier, 18)
    for d in range(1, 16):
        lane_copy(False, d).start()
    loads[1].wait()

    def scale_one(g, _):
        for k in range(NK):
            w1all[p, g, k] = (w1in[g, k].astype(F32) * s1_ref[g, k]).astype(BF)
        return 0

    lax.fori_loop(0, NB, scale_one, 0)
    for i in range(5):
        weight_copy(0, i).start()
    for cp in loads[2:]:
        cp.wait()
    for one in range(1, 4):
        for w in range(2):
            feature_copy(w, one, 0).start()
    for two in range(1, 4):
        for w in range(2):
            feature_copy(w, 0, two).start()
    w1all[:, :, NK] = jnp.zeros((8, NB, 16, 128), BF)
    w2all[:, :, NK] = jnp.zeros((8, NB, 16, 128), BF)

    def weights_on(w):
        weight_copy(w, 0).wait_recv()
        weight_copy(w, 5).start()
        weight_copy(w, 2).wait_recv()
        weight_copy(w, 6).start()
        weight_copy(w, 1).wait_recv()
        weight_copy(w, 7).start()
        weight_copy(w, 3).wait_recv()
        weight_copy(w, 8).start()

    def weights_last(w):
        weight_copy(w, 5).wait_recv()
        weight_copy(w, 6).wait_recv()
        weight_copy(w, 9).start()

    weights_on(0)
    for d in range(1, 16):
        lane_copy(False, d).wait_recv()
    rbuf[pl.ds(2 * t, 2)] = lanes[pl.ds(2 * t, 2)]

    def scale_two(g, _):
        i = home_lane_ref[g]
        for k in range(NK):
            w2all[p, g, k] = (rbuf[i, k].astype(F32) * s2_ref[g, k]).astype(BF)
        return 0

    lax.fori_loop(0, NB, scale_two, 0)
    for i in range(5):
        weight_copy(1, i).start()
    for one in range(1, 4):
        for w in range(2):
            feature_copy(w, one, 0).wait_recv()
            for two in range(1, 4):
                feature_copy(w, one, two).start()
    weights_last(0)
    for one in range(4):
        for two in range(1, 4):
            for w in range(2):
                feature_copy(w, one, two).wait_recv()
    for i in (4, 7, 8, 9):
        weight_copy(0, i).wait_recv()

    def project(g, _):
        w1c = jnp.concatenate([w1all[:, g, k].reshape(128, 128) for k in range(NK)], axis=0)
        xs = jnp.concatenate([xall[rows[g, k]] for k in range(NK)], axis=1)
        pre = jnp.dot(xs, w1c, preferred_element_type=F32)
        th = jnp.tanh(GELU_C * (pre + GELU_A * pre * pre * pre))
        act = (0.5 * pre * (1.0 + th)).astype(BF)
        slope[g] = 0.5 * (1.0 + th) + 0.5 * pre * (1.0 - th * th) * GELU_C * (
            1.0 + 3.0 * GELU_A * pre * pre
        )
        act_all[:, pl.ds(pl.multiple_of(g * 128, 128), 128)] = act
        dys = jnp.concatenate([dyall[cols[g, k]] for k in range(NK)], axis=1)
        gw2 = jnp.dot(act.T, dys, preferred_element_type=F32).astype(BF)
        for k in range(NK):
            g2s[:, :, g, k] = gw2[:, k * 128 : (k + 1) * 128].reshape(4, 2, 16, 128)
        return 0

    lax.fori_loop(0, HALF, project, 0)
    grad_copy(0, 6).start()
    weights_on(1)
    lax.fori_loop(HALF, NB, project, 0)
    grad_copy(0, 7).start()

    def pair_sum(w, chunk, h):
        own = grads[w]

        def body(g, _):
            own[chunk, c, g] = (own[chunk, c, g].astype(F32) + sib[chunk, g].astype(F32)).astype(BF)
            return 0

        lax.fori_loop(h * HALF, (h + 1) * HALF, body, 0)

    def pair_stage(w):
        grad_copy(w, 6).wait_recv()
        pair_sum(w, xo, 0)
        grad_copy(w, 0).start()
        pair_sum(w, xl, 0)
        grad_copy(w, 3).start()
        grad_copy(w, 7).wait_recv()
        pair_sum(w, xo, 1)
        grad_copy(w, 1).start()
        pair_sum(w, xr, 1)
        grad_copy(w, 2).start()
        pair_sum(w, xr, 0)
        pair_sum(w, xl, 1)
        pair_sum(w, x, 0)
        pair_sum(w, x, 1)

    def pass_stage(w):
        own = grads[w]
        grad_copy(w, 0).wait_recv()

        def right(g, _):
            own[xr, c, g] = (own[xr, c, g].astype(F32) + fwd[w, 0, g].astype(F32)).astype(BF)
            return 0

        lax.fori_loop(0, HALF, right, 0)
        grad_copy(w, 4).start()
        grad_copy(w, 1).wait_recv()

        def left(g, _):
            own[xl, c, g + HALF] = (
                own[xl, c, g + HALF].astype(F32) + fwd[w, 1, g].astype(F32)
            ).astype(BF)
            return 0

        lax.fori_loop(0, HALF, left, 0)
        grad_copy(w, 5).start()

    def last_stage(w, out, scale):
        own = grads[w]
        for i in (2, 3, 4, 5):
            grad_copy(w, i).wait_recv()

        def body(g, _):
            for k in range(NK):
                total = own[x, c, g, k].astype(F32) + fin[w, 0, g, k].astype(F32)
                total = total + fin[w, 1, g, k].astype(F32)
                out(g, k, (total * scale[g, k]).astype(BF))
            return 0

        lax.fori_loop(0, NB, body, 0)

    weights_last(1)
    pair_stage(0)
    pl.semaphore_signal(free_sem, inc=1, device_id=(sp, t), device_id_type=MESH)

    def flip(j, _):
        xt[j] = xall[j].T
        return 0

    lax.fori_loop(0, 48, flip, 0)
    for i in (4, 7, 8, 9):
        weight_copy(1, i).wait_recv()

    def hidden(g, _):
        w2c = jnp.concatenate([w2all[:, g, k].reshape(128, 128) for k in range(NK)], axis=1)
        dys = jnp.concatenate([dyall[cols[g, k]] for k in range(NK)], axis=1)
        dact = lax.dot_general(dys, w2c, nt, preferred_element_type=F32).astype(BF)
        dpre = (dact.astype(F32) * slope[g]).astype(BF)
        dpre_all[:, pl.ds(pl.multiple_of(g * 128, 128), 128)] = dpre
        for k in range(NK):
            gw1 = jnp.dot(xt[rows[g, k]], dpre, preferred_element_type=F32).astype(BF)
            g1s[:, :, g, k] = gw1.reshape(4, 2, 16, 128)
        return 0

    lax.fori_loop(0, HALF, hidden, 0)
    pl.semaphore_wait(free_sem, 1)
    grad_copy(1, 6).start()
    lax.fori_loop(HALF, NB, hidden, 0)
    grad_copy(1, 7).start()
    pass_stage(0)

    def mix(row):
        def body(i, _):
            j = 12 * row + 2 * i
            panel = jnp.concatenate(
                [
                    jnp.concatenate(
                        [w2all[:, g, kv2[j + b, g]].reshape(128, 128) for g in range(NB)], axis=0
                    )
                    for b in range(2)
                ],
                axis=1,
            )
            res = jnp.dot(act_all[...], panel, preferred_element_type=F32).astype(BF)
            for b in range(2):
                at = 2 * i + b
                m_part[row, at // 3, at % 3] = res[:, b * 128 : (b + 1) * 128]
            return 0

        lax.fori_loop(0, 6, body, 0)

    def back(col):
        def body(i, _):
            at = (2 * i, 2 * i + 1)
            panel = jnp.concatenate(
                [
                    jnp.concatenate(
                        [
                            w1all[:, g, kv1[12 * (a // 3) + 3 * col + a % 3, g]].reshape(128, 128)
                            for g in range(NB)
                        ],
                        axis=1,
                    )
                    for a in at
                ],
                axis=0,
            )
            res = lax.dot_general(dpre_all[...], panel, nt, preferred_element_type=F32).astype(BF)
            for b, a in enumerate(at):
                d_part[a // 3, col, a % 3] = res[:, b * 128 : (b + 1) * 128]
            return 0

        lax.fori_loop(0, 6, body, 0)

    for d in range(1, 4):
        mix((y + d) % 4)
        part_copy(0, 0, d).start()
        back((z + d) % 4)
        part_copy(1, 0, d).start()
        if d == 1:
            pair_stage(1)
    mix(y)
    back(z)

    def keep_two(g, k, value):
        g2s[x, c, g, k] = value

    last_stage(0, keep_two, s2_ref)
    for d in range(1, 16):
        lane_copy(False, d).wait_send()

    def lanes_back(i, _):
        s = home_local_ref[i]
        lanes[i] = g2s[x, c, s]
        return 0

    lax.fori_loop(0, 32, lanes_back, 0)
    for d in range(1, 16):
        lane_copy(True, d).start()
    rback[pl.ds(2 * t, 2)] = lanes[pl.ds(2 * t, 2)]
    for w in range(2):
        for d in range(1, 4):
            part_copy(w, 0, d).wait_recv()
        part = parts[w]

        def add_four(i, _):
            a, b = i // 3, i % 3
            here = (y, a) if w == 0 else (a, z)
            total = part[here[0], here[1], b].astype(F32)
            for d in range(3):
                total = total + f_buf[w, d, a, b].astype(F32)
            part[here[0], here[1], b] = total.astype(BF)
            return 0

        lax.fori_loop(0, 12, add_four, 0)
        for d in range(1, 4):
            part_copy(w, 1, d).start()
    pass_stage(1)
    for w, out in ((0, mixed), (1, dxo)):
        for d in range(1, 4):
            part_copy(w, 1, d).wait_recv()
        for b in range(3):
            total = parts[w][y, z, b].astype(F32)
            for d in range(3):
                total = total + f_fin[w, d, b].astype(F32)
            out[:, b * 128 : (b + 1) * 128] = total.astype(BF)
    for d in range(1, 16):
        lane_copy(True, d).wait_recv()

    def slot_out(s, _):
        i = slot_lane_ref[s]
        o2[s] = jnp.where(slot_live_ref[s] > 0, rback[i], jnp.zeros_like(rback[i]))
        return 0

    lax.fori_loop(0, CAP, slot_out, 0)

    def keep_one(g, k, value):
        o1[g, k] = value

    last_stage(1, keep_one, s1_ref)
    for d in range(1, 16):
        lane_copy(True, d).wait_send()
    for w in range(2):
        for i in range(10):
            weight_copy(w, i).wait_send()
        for one in range(4):
            for two in range(4):
                if one or two:
                    feature_copy(w, one, two).wait_send()
        for i in range(8):
            grad_copy(w, i).wait_send()
        for step in range(2):
            for d in range(1, 4):
                part_copy(w, step, d).wait_send()


def route_tables(owner, rank):
    index = jnp.arange(192, dtype=jnp.int32)
    source = index // NB
    earlier = index[None, :] < index[:, None]
    same_dest = owner[None, :] == owner[:, None]
    same_src = source[None, :] == source[:, None]
    slot = jnp.sum((earlier & same_dest).astype(jnp.int32), axis=1)
    pair = jnp.sum((earlier & same_dest & same_src).astype(jnp.int32), axis=1)
    mine_first = rank * NB
    mine_owner = lax.dynamic_slice(owner, (mine_first,), (NB,))
    mine_pair = lax.dynamic_slice(pair, (mine_first,), (NB,))
    mine_slot = lax.dynamic_slice(slot, (mine_first,), (NB,))
    home_lane = mine_owner * 2 + mine_pair
    home_q = mine_owner * CAP + mine_slot
    lane = jnp.arange(32, dtype=jnp.int32)
    mine_lane = jnp.where(owner == rank, source * 2 + pair, -1)
    own_slot = jnp.sum(jnp.where(lane[:, None] == mine_lane[None, :], slot[None, :], 0), axis=1)
    home_local = jnp.sum(
        jnp.where(
            lane[:, None] == home_lane[None, :], jnp.arange(NB, dtype=jnp.int32)[None, :], 0
        ),
        axis=1,
    )
    mine_at = jnp.where(owner == rank, slot, -1)
    hit = jnp.arange(CAP, dtype=jnp.int32)[:, None] == mine_at[None, :]
    slot_lane = jnp.sum(jnp.where(hit, (source * 2 + pair)[None, :], 0), axis=1)
    slot_live = jnp.any(hit, axis=1).astype(jnp.int32)
    return home_lane, home_q, own_slot, home_local, slot_lane, slot_live


VM = pl.BlockSpec(memory_space=pltpu.VMEM)
SM = pl.BlockSpec(memory_space=pltpu.SMEM)
ANY = pl.BlockSpec(memory_space=pl.ANY)
SHARD = (NB, NK, 16, 128)
LANES = (32, NK, 16, 128)


def inverse(index):
    k = jnp.arange(NK, dtype=jnp.int32)
    hit = index[None, :, :] == jnp.arange(48, dtype=jnp.int32)[:, None, None]
    return NK + jnp.sum(jnp.where(hit, k[None, None, :] - NK, 0), axis=2)


def local(tokens, cotangent, w1_blocks, w1_rows, w1_scale, w2_blocks, w2_cols, w2_scale, owner):
    rank = lax.axis_index("tensor")
    home_lane, home_q, own_slot, home_local, slot_lane, slot_live = route_tables(owner, rank)
    rows = lax.dynamic_slice(w1_rows, (rank * NB, 0), (NB, NK))
    scale_one = lax.dynamic_slice(w1_scale, (rank * NB, 0), (NB, NK))
    cols = w2_cols[home_q]
    scale_two = w2_scale[home_q]
    dma = pltpu.SemaphoreType.DMA
    part = (4, 4, 3, 192, 128)
    return pl.pallas_call(
        layer_kernel,
        out_shape=[
            jax.ShapeDtypeStruct((192, 384), BF),
            jax.ShapeDtypeStruct((192, 384), BF),
            jax.ShapeDtypeStruct(SHARD, BF),
            jax.ShapeDtypeStruct((CAP, NK, 16, 128), BF),
        ],
        in_specs=[ANY] * 4 + [SM] * 11,
        out_specs=[VM] * 4,
        scratch_shapes=[
            pltpu.VMEM(SHARD, BF),
            pltpu.VMEM((CAP, NK, 16, 128), BF),
            pltpu.VMEM((48, 192, 128), BF),
            pltpu.VMEM((48, 192, 128), BF),
            pltpu.VMEM((8, NB, NK + 1, 16, 128), BF),
            pltpu.VMEM((8, NB, NK + 1, 16, 128), BF),
            pltpu.VMEM(LANES, BF),
            pltpu.VMEM(LANES, BF),
            pltpu.VMEM(LANES, BF),
            pltpu.VMEM((48, 128, 192), BF),
            pltpu.VMEM((NB, 192, 128), F32),
            pltpu.VMEM((192, NB * 128), BF),
            pltpu.VMEM((192, NB * 128), BF),
            pltpu.VMEM((4, 2) + SHARD, BF),
            pltpu.VMEM((4, 2) + SHARD, BF),
            pltpu.VMEM((4,) + SHARD, BF),
            pltpu.VMEM((2, 2, HALF, NK, 16, 128), BF),
            pltpu.VMEM((2, 2) + SHARD, BF),
            pltpu.VMEM(part, BF),
            pltpu.VMEM(part, BF),
            pltpu.VMEM((2, 3, 4, 3, 192, 128), BF),
            pltpu.VMEM((2, 3, 3, 192, 128), BF),
            dma((16,)),
            dma((16,)),
            dma((16,)),
            dma((16,)),
            dma((2, 10)),
            dma((2, 10)),
            dma((2, 4, 4)),
            dma((2, 4, 4)),
            dma((2, 8)),
            dma((2, 8)),
            dma((2, 2, 4)),
            dma((2, 2, 4)),
            dma((8,)),
            pltpu.SemaphoreType.REGULAR,
        ],
        compiler_params=pltpu.CompilerParams(
            collective_id=0, has_side_effects=True, vmem_limit_bytes=63 << 20
        ),
    )(
        tokens,
        cotangent,
        w1_blocks,
        w2_blocks,
        scale_one,
        scale_two,
        rows,
        cols,
        inverse(rows),
        inverse(cols),
        own_slot,
        home_lane,
        home_local,
        slot_lane,
        slot_live,
    )


def solution(mesh):
    in_specs = (
        P("dp", "tensor"),
        P("dp", "tensor"),
        P("tensor", None, "dp", None),
        P(),
        P(),
        P("tensor", None, "dp", None),
        P(),
        P(),
        P(),
    )
    out_specs = (
        P("dp", "tensor"),
        P("dp", "tensor"),
        P("tensor", None, "dp", None),
        P("tensor", None, "dp", None),
    )
    return jax.shard_map(local, mesh=mesh, in_specs=in_specs, out_specs=out_specs, check_vma=False)
```

time: 586 us -> 187 us (0.32); the launches traced: 578 us -> 186 us
  waiting for transfers between devices: 280 us -> 0 us
  Pallas kernels: 0 us -> 168 us
  other arithmetic: 130 us -> 5.95 us
  matrix products: 70.2 us -> 0 us
  local copies, waits for them, and re-layouts: 67.6 us -> 11.6 us
  starting transfers between devices: 15.4 us -> 0 us
  between operations: 14.8 us -> 0.73 us
    pallas_call x0 -> x1, Pallas kernels: none -> 168 us  [local(): pl.pallas_call(layer_kernel, out_shape=[jax.ShapeDtypeStruct((192, 384),...]
    scatter-add x2 -> x0, other arithmetic: 117 us -> none  [place_blocks(): empty.at[:, targets.reshape(-1)].add(flat)]
    reduce_scatter x2 -> x0, waiting for transfers between devices: 98.6 us -> none  [the longest x1 57.2 us: local(): lax.psum_scatter(gw_two.astype(jnp.bfloat16), 'dp', scatter_dimension=2,...]
    all_gather x4 -> x0, waiting for transfers between devices: 91.5 us -> none  [the longest x1 44.2 us: local(): lax.all_gather(tokens, 'tensor', axis=1, tiled=True)]
    dot_general x6 -> x0, matrix products: 70.2 us -> none  [the longest x1 16.1 us: local(): jnp.einsum('tsi,sbio->tsbo', act_here, weff_two, preferred_element_type=j...]
    all_to_all x2 -> x0, waiting for transfers between devices: 50.3 us -> none  [the longest x1 26.7 us: local(): lax.all_to_all(pick(dact_here, own_slot, own_live, 1), 'tensor', split_ax...]
    unnamed x10 -> x0, waiting for transfers between devices: 39.5 us -> none
    gather x15 -> x2, local copies, waits for them, and re-layouts: 31.6 us -> 1.72 us  [the longest x1 1.15 us: local(): scale_two = w2_scale[home_q]]
  transfers between devices with their start and end apart: 10 -> 0, of which waited for: 8 -> 0; matrix products, arithmetic and copies ran while one was open for 46% -> 0% of each run, Pallas kernels for 0% -> 0%
where the time goes in v2:
time: 187 us; the launch traced here: 186 us
  Pallas kernels  168 us (90%)
  local copies, waits for them, and re-layouts  11.6 us (6%)
  other arithmetic  5.95 us (3%)
    pallas_call x1, Pallas kernels, local(): pl.pallas_call(layer_kernel, out_shape=[jax.ShapeDtypeStruct((192, 384),...  168 us
    unnamed x18, local copies, waits for them, and re-layouts  8.84 us

profile of v2, /device:TPU:0, one launch (start us, length us, event | category | flops | bytes accessed | tf_op | source)
XLA Modules:
  0.0 185.8 jit_solution(9772009922422100055)
XLA Ops:
  0.6 0.0 copy-start
  0.7 1.0 convert_reduce_fusion
  1.7 0.8 dynamic-slice_add_fusion
  2.4 0.0 copy-start.4
  2.4 0.7 select_reduce_fusion.4.home_local_ref
  3.1 0.7 broadcast_select_fusion
  3.8 0.6 select_reduce_fusion.2.own_slot_ref
  4.4 0.7 select_reduce_fusion.3.slot_lane_ref
  5.1 0.1 fusion.1
  5.2 0.6 convert_element_type.11.slot_live_ref
  5.8 0.0 copy-done
  5.8 0.1 constant_dynamic-slice_fusion
  5.9 0.1 copy.32.rows
  6.0 0.0 copy-start.3
  6.0 0.8 constant_dynamic-slice_fusion.1
  6.8 0.7 copy.31.s1_ref
  7.5 0.8 copy.26
  8.4 0.6 gather_fusion.1
  8.9 0.0 copy-start.2
  8.9 0.2 select_reduce_fusion
  9.1 0.1 copy.29
  9.2 0.1 copy.27
  9.3 0.6 broadcast_add_fusion
  9.9 0.8 copy.24
  10.8 1.2 gather_fusion
  11.9 0.0 copy-done.4
  11.9 0.0 copy-done.3
  11.9 0.0 copy-done.2
  11.9 167.5 %shard_map.120 = (bf16[192,384]{1,0:T(8,128)(2,1)}, bf16[192,384]{1,0:T(8,128)(2,1)}, bf16[12,15,16,128]{3,2,1,0:T(8,128)(2,1)}, bf16[18,15,16,128]{3,2,1,0:T(8,128)(2,1)}) custom-call(bf16[192,384]{1,0:T(8,128)(2,1)} %tok_ref.1, bf16[192,384]{1,0:T(8,128)(2,1)} %cot_ref.1, bf16[12,15,16,128]{3,2,1,0:T(8,128)(2,1)} %w1_ref.1, ...), custom_call_target="tpu_custom_call" | custom-call | tf_op jit(solution)/shard_map/pallas_call | solution.py:565
  179.4 0.0 copy-start.1
  179.4 1.7 copy.37
  181.1 1.6 copy.38
  182.7 2.1 %copy.39 = bf16[12,15,16,128]{3,2,1,0:T(8,128)(2,1)} copy(bf16[12,15,16,128]{3,2,1,0:T(8,128)(2,1)} %get-tuple-element.21) | data formatting | bytes 1474560
  184.8 0.0 copy-done.1
  184.8 1.0 copy.40
  (3 shorter events, 0.0 us)
Async XLA Ops:
  0.6 5.2 %copy-start = (s32[192,15]{0,1:T(8,128)S(1)}, s32[192,15]{0,1:T(8,128)}, u32[]{:S(2)}) copy-start(s32[192,15]{0,1:T(8,128)} %param.12) | copy-start | bytes 34564
  2.4 9.5 %copy-start.4 = (s32[12]{0:T(128)}, s32[12]{0:T(128)S(1)}, u32[]{:S(2)}) copy-start(s32[12]{0:T(128)S(1)} %get-tuple-element.11.home_lane_ref) | copy-start | bytes 148
  6.0 5.9 %copy-start.3 = (s32[12,15]{1,0:T(8,128)}, s32[12,15]{1,0:T(8,128)S(1)}, u32[]{:S(2)}) copy-start(s32[12,15]{1,0:T(8,128)S(1)} %copy.32.rows) | copy-start | bytes 2164
  8.9 3.0 %copy-start.2 = (s32[12,15]{1,0:T(8,128)}, s32[12,15]{1,0:T(8,128)S(1)}, u32[]{:S(2)}) copy-start(s32[12,15]{1,0:T(8,128)S(1)} %gather_fusion.1) | copy-start | bytes 2164
  179.4 5.4 %copy-start.1 = (bf16[18,15,16,128]{3,2,1,0:T(8,128)(2,1)S(1)}, bf16[18,15,16,128]{3,2,1,0:T(8,128)(2,1)}, u32[]{:S(2)}) copy-start(bf16[18,15,16,128]{3,2,1,0:T(8,128)(2,1)} %get-tuple-element.22) | copy-start | bytes 3317764

commit v3 on v2

--- a/solution.py
+++ b/solution.py
@@ -24,9 +24,9 @@
 
 def enter(p, t, x, c, y, z):
     barrier = pltpu.get_barrier_semaphore()
-    for d in range(1, 16):
-        peer = ((y + d // 4) % 4) * 4 + (z + d % 4) % 4
-        pl.semaphore_signal(barrier, inc=1, device_id=(p, peer), device_id_type=MESH)
+    for d in range(1, 4):
+        for peer in (((y + d) % 4) * 4 + z, y * 4 + (z + d) % 4):
+            pl.semaphore_signal(barrier, inc=1, device_id=(p, peer), device_id_type=MESH)
     for q in (2 * ((x + 1) % 4) + c, 2 * ((x + 3) % 4) + c, 2 * x + 1 - c):
         pl.semaphore_signal(barrier, inc=1, device_id=(q, t), device_id_type=MESH)
     return barrier
@@ -61,6 +61,7 @@
     lanes,
     rbuf,
     rback,
+    middle,
     xt,
     slope,
     act_all,
@@ -76,8 +77,6 @@
     f_fin,
     a_send,
     a_recv,
-    b_send,
-    b_recv,
     w_send,
     w_recv,
     x_send,
@@ -100,18 +99,49 @@
     weights = (w1all, w2all)
     grads = (g2s, g1s)
     parts = (m_part, d_part)
+    landed = (rbuf, rback)
     nt = (((1,), (1,)), ((), ()))
 
-    def lane_copy(back, d):
-        peer = ((y + d // 4) % 4) * 4 + (z + d % 4) % 4
+    def lane_copy(trip, j, step, d):
+        along_y = (j == 0) == (step == 0)
+        peer_y, peer_z = ((y + d) % 4, z) if along_y else (y, (z + d) % 4)
+        src = lanes.at[j] if step == 0 else middle.at[trip, j]
+        dst = middle.at[trip, j] if step == 0 else landed[trip].at[j]
         return pltpu.make_async_remote_copy(
-            lanes.at[pl.ds(2 * peer, 2)],
-            (rback if back else rbuf).at[pl.ds(2 * t, 2)],
-            (b_send if back else a_send).at[d],
-            (b_recv if back else a_recv).at[d],
-            device_id=(p, peer),
+            src.at[peer_y] if along_y else src.at[:, peer_z],
+            dst.at[y] if along_y else dst.at[:, z],
+            a_send.at[trip, j, step, d],
+            a_recv.at[trip, j, step, d],
+            device_id=(p, peer_y * 4 + peer_z),
             device_id_type=MESH,
         )
+
+    def lanes_go(trip):
+        for d in (2, 1, 3):
+            for j in range(2):
+                lane_copy(trip, j, 0, d).start()
+        middle[trip, 0, y] = lanes[0, y]
+        middle[trip, 1, :, z] = lanes[1, :, z]
+
+    def lanes_turn(trip):
+        for j in range(2):
+            for d in range(1, 4):
+                lane_copy(trip, j, 0, d).wait_recv()
+            for d in (2, 1, 3):
+                lane_copy(trip, j, 1, d).start()
+        landed[trip][0, :, z] = middle[trip, 0, :, z]
+        landed[trip][1, y] = middle[trip, 1, y]
+
+    def lanes_end(trip):
+        for j in range(2):
+            for d in range(1, 4):
+                lane_copy(trip, j, 1, d).wait_recv()
+
+    def lanes_sent(trip):
+        for j in range(2):
+            for step in range(2):
+                for d in range(1, 4):
+                    lane_copy(trip, j, step, d).wait_send()
 
     def weight_copy(w, i):
         who, part, dev = (
@@ -131,21 +161,24 @@
             ref, ref, w_send.at[w, i], w_recv.at[w, i], device_id=(dev, t), device_id_type=MESH
         )
 
-    def feature_copy(w, one, two):
-        if two == 0:
-            holder = t
-            ay, az = (one, 0) if w == 0 else (0, one)
+    def feature_copy(w, group, i):
+        along_y = (w == 0) == (group == 0)
+        came = 0 if group == 0 else group - 1
+        on = (0, 0, 1, 3)[i]
+        if along_y:
+            holder = ((y + 4 - on) % 4) * 4 + (z + 4 - came) % 4
         else:
-            by, bz = (one, 0) if w == 0 else (0, one)
-            holder = ((y + 4 - by) % 4) * 4 + (z + 4 - bz) % 4
-            ay, az = (0, two) if w == 0 else (two, 0)
-        peer = ((y + ay) % 4) * 4 + (z + az) % 4
+            holder = ((y + 4 - came) % 4) * 4 + (z + 4 - on) % 4
+        d = (1, 3, 1, 3)[i]
+        peer = ((y + d) % 4) * 4 + z if along_y else y * 4 + (z + d) % 4
         ref = feats[w].at[pl.ds(3 * holder, 3)]
+        if i >= 2:
+            ref = ref.at[:, pl.ds(96 * (i - 2), 96)]
         return pltpu.make_async_remote_copy(
             ref,
             ref,
-            x_send.at[w, one, two],
-            x_recv.at[w, one, two],
+            x_send.at[w, group, i],
+            x_recv.at[w, group, i],
             device_id=(p, peer),
             device_id_type=MESH,
         )
@@ -203,13 +236,12 @@
 
     def lanes_out(i, _):
         s = own_slot_ref[i]
-        lanes[i] = w2in[s]
+        lanes[i // 16, (i // 4) % 4, i % 4] = w2in[s]
         return 0
 
     lax.fori_loop(0, 32, lanes_out, 0)
-    pl.semaphore_wait(barrier, 18)
-    for d in range(1, 16):
-        lane_copy(False, d).start()
+    pl.semaphore_wait(barrier, 9)
+    lanes_go(0)
     loads[1].wait()
 
     def scale_one(g, _):
@@ -220,16 +252,10 @@
     lax.fori_loop(0, NB, scale_one, 0)
     for i in range(5):
         weight_copy(0, i).start()
+    w1all[:, :, NK] = jnp.zeros((8, NB, 16, 128), BF)
+    w2all[:, :, NK] = jnp.zeros((8, NB, 16, 128), BF)
     for cp in loads[2:]:
         cp.wait()
-    for one in range(1, 4):
-        for w in range(2):
-            feature_copy(w, one, 0).start()
-    for two in range(1, 4):
-        for w in range(2):
-            feature_copy(w, 0, two).start()
-    w1all[:, :, NK] = jnp.zeros((8, NB, 16, 128), BF)
-    w2all[:, :, NK] = jnp.zeros((8, NB, 16, 128), BF)
 
     def weights_on(w):
         weight_copy(w, 0).wait_recv()
@@ -246,30 +272,52 @@
         weight_copy(w, 6).wait_recv()
         weight_copy(w, 9).start()
 
+    lanes_turn(0)
+    for group in (0, 1):
+        for w in range(2):
+            for i in range(2):
+                feature_copy(w, group, i).start()
     weights_on(0)
-    for d in range(1, 16):
-        lane_copy(False, d).wait_recv()
-    rbuf[pl.ds(2 * t, 2)] = lanes[pl.ds(2 * t, 2)]
+    lanes_end(0)
 
     def scale_two(g, _):
         i = home_lane_ref[g]
         for k in range(NK):
-            w2all[p, g, k] = (rbuf[i, k].astype(F32) * s2_ref[g, k]).astype(BF)
+            w2all[p, g, k] = (rbuf[i // 16, (i // 4) % 4, i % 4, k].astype(F32) * s2_ref[g, k]).astype(BF)
         return 0
 
     lax.fori_loop(0, NB, scale_two, 0)
     for i in range(5):
         weight_copy(1, i).start()
-    for one in range(1, 4):
+
+    def feature_on(w, group):
+        for i in range(2):
+            feature_copy(w, group, i).wait_recv()
+            feature_copy(w, group, i + 2).start()
+            if group == 0:
+                for k in range(2):
+                    feature_copy(w, (2, 4)[i], k).start()
+
+    for w in range(2):
+        feature_on(w, 0)
+    for w in range(2):
+        feature_on(w, 1)
+    weights_last(0)
+    for w in range(2):
+        for i in (2, 3):
+            feature_copy(w, 0, i).wait_recv()
+        for k in range(2):
+            feature_copy(w, 3, k).start()
+    for group in (2, 4):
         for w in range(2):
-            feature_copy(w, one, 0).wait_recv()
-            for two in range(1, 4):
-                feature_copy(w, one, two).start()
-    weights_last(0)
-    for one in range(4):
-        for two in range(1, 4):
-            for w in range(2):
-                feature_copy(w, one, two).wait_recv()
+            feature_on(w, group)
+    weights_on(1)
+    for w in range(2):
+        feature_on(w, 3)
+    for group in range(1, 5):
+        for w in range(2):
+            for i in (2, 3):
+                feature_copy(w, group, i).wait_recv()
     for i in (4, 7, 8, 9):
         weight_copy(0, i).wait_recv()
 
@@ -291,7 +339,7 @@
 
     lax.fori_loop(0, HALF, project, 0)
     grad_copy(0, 6).start()
-    weights_on(1)
+    weights_last(1)
     lax.fori_loop(HALF, NB, project, 0)
     grad_copy(0, 7).start()
 
@@ -354,36 +402,6 @@
             return 0
 
         lax.fori_loop(0, NB, body, 0)
-
-    weights_last(1)
-    pair_stage(0)
-    pl.semaphore_signal(free_sem, inc=1, device_id=(sp, t), device_id_type=MESH)
-
-    def flip(j, _):
-        xt[j] = xall[j].T
-        return 0
-
-    lax.fori_loop(0, 48, flip, 0)
-    for i in (4, 7, 8, 9):
-        weight_copy(1, i).wait_recv()
-
-    def hidden(g, _):
-        w2c = jnp.concatenate([w2all[:, g, k].reshape(128, 128) for k in range(NK)], axis=1)
-        dys = jnp.concatenate([dyall[cols[g, k]] for k in range(NK)], axis=1)
-        dact = lax.dot_general(dys, w2c, nt, preferred_element_type=F32).astype(BF)
-        dpre = (dact.astype(F32) * slope[g]).astype(BF)
-        dpre_all[:, pl.ds(pl.multiple_of(g * 128, 128), 128)] = dpre
-        for k in range(NK):
-            gw1 = jnp.dot(xt[rows[g, k]], dpre, preferred_element_type=F32).astype(BF)
-            g1s[:, :, g, k] = gw1.reshape(4, 2, 16, 128)
-        return 0
-
-    lax.fori_loop(0, HALF, hidden, 0)
-    pl.semaphore_wait(free_sem, 1)
-    grad_copy(1, 6).start()
-    lax.fori_loop(HALF, NB, hidden, 0)
-    grad_copy(1, 7).start()
-    pass_stage(0)
 
     def mix(row):
         def body(i, _):
@@ -428,32 +446,62 @@
 
         lax.fori_loop(0, 6, body, 0)
 
-    for d in range(1, 4):
+    pair_stage(0)
+    pl.semaphore_signal(free_sem, inc=1, device_id=(sp, t), device_id_type=MESH)
+
+    def flip(j, _):
+        xt[j] = xall[j].T
+        return 0
+
+    lax.fori_loop(0, 48, flip, 0)
+    for i in (4, 7, 8, 9):
+        weight_copy(1, i).wait_recv()
+
+    for d in (2, 1, 3):
         mix((y + d) % 4)
         part_copy(0, 0, d).start()
+
+    def hidden(g, _):
+        w2c = jnp.concatenate([w2all[:, g, k].reshape(128, 128) for k in range(NK)], axis=1)
+        dys = jnp.concatenate([dyall[cols[g, k]] for k in range(NK)], axis=1)
+        dact = lax.dot_general(dys, w2c, nt, preferred_element_type=F32).astype(BF)
+        dpre = (dact.astype(F32) * slope[g]).astype(BF)
+        dpre_all[:, pl.ds(pl.multiple_of(g * 128, 128), 128)] = dpre
+        for k in range(NK):
+            gw1 = jnp.dot(xt[rows[g, k]], dpre, preferred_element_type=F32).astype(BF)
+            g1s[:, :, g, k] = gw1.reshape(4, 2, 16, 128)
+        return 0
+
+    lax.fori_loop(0, HALF, hidden, 0)
+    pl.semaphore_wait(free_sem, 1)
+    grad_copy(1, 6).start()
+    lax.fori_loop(HALF, NB, hidden, 0)
+    grad_copy(1, 7).start()
+    pass_stage(0)
+    pair_stage(1)
+    back((z + 2) % 4)
+    part_copy(1, 0, 2).start()
+
+    def keep_two(g, k, value):
+        g2s[x, c, g, k] = value
+
+    last_stage(0, keep_two, s2_ref)
+    lanes_sent(0)
+
+    def lanes_back(i, _):
+        s = home_local_ref[i]
+        lanes[i // 16, (i // 4) % 4, i % 4] = g2s[x, c, s]
+        return 0
+
+    lax.fori_loop(0, 32, lanes_back, 0)
+    lanes_go(1)
+    for d in (1, 3):
         back((z + d) % 4)
         part_copy(1, 0, d).start()
-        if d == 1:
-            pair_stage(1)
+    pass_stage(1)
     mix(y)
+    lanes_turn(1)
     back(z)
-
-    def keep_two(g, k, value):
-        g2s[x, c, g, k] = value
-
-    last_stage(0, keep_two, s2_ref)
-    for d in range(1, 16):
-        lane_copy(False, d).wait_send()
-
-    def lanes_back(i, _):
-        s = home_local_ref[i]
-        lanes[i] = g2s[x, c, s]
-        return 0
-
-    lax.fori_loop(0, 32, lanes_back, 0)
-    for d in range(1, 16):
-        lane_copy(True, d).start()
-    rback[pl.ds(2 * t, 2)] = lanes[pl.ds(2 * t, 2)]
     for w in range(2):
         for d in range(1, 4):
             part_copy(w, 0, d).wait_recv()
@@ -471,7 +519,6 @@
         lax.fori_loop(0, 12, add_four, 0)
         for d in range(1, 4):
             part_copy(w, 1, d).start()
-    pass_stage(1)
     for w, out in ((0, mixed), (1, dxo)):
         for d in range(1, 4):
             part_copy(w, 1, d).wait_recv()
@@ -480,12 +527,12 @@
             for d in range(3):
                 total = total + f_fin[w, d, b].astype(F32)
             out[:, b * 128 : (b + 1) * 128] = total.astype(BF)
-    for d in range(1, 16):
-        lane_copy(True, d).wait_recv()
+    lanes_end(1)
 
     def slot_out(s, _):
         i = slot_lane_ref[s]
-        o2[s] = jnp.where(slot_live_ref[s] > 0, rback[i], jnp.zeros_like(rback[i]))
+        got = rback[i // 16, (i // 4) % 4, i % 4]
+        o2[s] = jnp.where(slot_live_ref[s] > 0, got, jnp.zeros_like(got))
         return 0
 
     lax.fori_loop(0, CAP, slot_out, 0)
@@ -494,15 +541,13 @@
         o1[g, k] = value
 
     last_stage(1, keep_one, s1_ref)
-    for d in range(1, 16):
-        lane_copy(True, d).wait_send()
+    lanes_sent(1)
     for w in range(2):
         for i in range(10):
             weight_copy(w, i).wait_send()
-        for one in range(4):
-            for two in range(4):
-                if one or two:
-                    feature_copy(w, one, two).wait_send()
+        for group in range(5):
+            for i in range(4):
+                feature_copy(w, group, i).wait_send()
         for i in range(8):
             grad_copy(w, i).wait_send()
         for step in range(2):
@@ -522,10 +567,10 @@
     mine_owner = lax.dynamic_slice(owner, (mine_first,), (NB,))
     mine_pair = lax.dynamic_slice(pair, (mine_first,), (NB,))
     mine_slot = lax.dynamic_slice(slot, (mine_first,), (NB,))
-    home_lane = mine_owner * 2 + mine_pair
+    home_lane = mine_pair * 16 + mine_owner
     home_q = mine_owner * CAP + mine_slot
     lane = jnp.arange(32, dtype=jnp.int32)
-    mine_lane = jnp.where(owner == rank, source * 2 + pair, -1)
+    mine_lane = jnp.where(owner == rank, pair * 16 + source, -1)
     own_slot = jnp.sum(jnp.where(lane[:, None] == mine_lane[None, :], slot[None, :], 0), axis=1)
     home_local = jnp.sum(
         jnp.where(
@@ -535,7 +580,7 @@
     )
     mine_at = jnp.where(owner == rank, slot, -1)
     hit = jnp.arange(CAP, dtype=jnp.int32)[:, None] == mine_at[None, :]
-    slot_lane = jnp.sum(jnp.where(hit, (source * 2 + pair)[None, :], 0), axis=1)
+    slot_lane = jnp.sum(jnp.where(hit, (pair * 16 + source)[None, :], 0), axis=1)
     slot_live = jnp.any(hit, axis=1).astype(jnp.int32)
     return home_lane, home_q, own_slot, home_local, slot_lane, slot_live
 
@@ -544,7 +589,7 @@
 SM = pl.BlockSpec(memory_space=pltpu.SMEM)
 ANY = pl.BlockSpec(memory_space=pl.ANY)
 SHARD = (NB, NK, 16, 128)
-LANES = (32, NK, 16, 128)
+LANES = (2, 4, 4, NK, 16, 128)
 
 
 def inverse(index):
@@ -582,6 +627,7 @@
             pltpu.VMEM(LANES, BF),
             pltpu.VMEM(LANES, BF),
             pltpu.VMEM(LANES, BF),
+            pltpu.VMEM((2,) + LANES, BF),
             pltpu.VMEM((48, 128, 192), BF),
             pltpu.VMEM((NB, 192, 128), F32),
             pltpu.VMEM((192, NB * 128), BF),
@@ -595,14 +641,12 @@
             pltpu.VMEM(part, BF),
             pltpu.VMEM((2, 3, 4, 3, 192, 128), BF),
             pltpu.VMEM((2, 3, 3, 192, 128), BF),
-            dma((16,)),
-            dma((16,)),
-            dma((16,)),
-            dma((16,)),
+            dma((2, 2, 2, 4)),
+            dma((2, 2, 2, 4)),
             dma((2, 10)),
             dma((2, 10)),
-            dma((2, 4, 4)),
-            dma((2, 4, 4)),
+            dma((2, 5, 4)),
+            dma((2, 5, 4)),
             dma((2, 8)),
             dma((2, 8)),
             dma((2, 2, 4)),
@@ -611,7 +655,7 @@
             pltpu.SemaphoreType.REGULAR,
         ],
         compiler_params=pltpu.CompilerParams(
-            collective_id=0, has_side_effects=True, vmem_limit_bytes=63 << 20
+            collective_id=0, has_side_effects=True, vmem_limit_bytes=(64 << 20) - (64 << 10)
         ),
     )(
         tokens,

time: 187 us -> 179 us (0.957)
  Pallas kernels: 168 us -> 159 us
    pallas_call x1, Pallas kernels: 168 us -> 159 us  [local(): pl.pallas_call(layer_kernel, out_shape=[jax.ShapeDtypeStruct((192, 384),...]
    unnamed x18 -> x16, local copies, waits for them, and re-layouts: 8.84 us -> 9.33 us
where the time goes in v3:
time: 179 us; the launch traced here: 178 us
  Pallas kernels  159 us (89%)
  local copies, waits for them, and re-layouts  12.8 us (7%)
  other arithmetic  5.95 us (3%)
    pallas_call x1, Pallas kernels, local(): pl.pallas_call(layer_kernel, out_shape=[jax.ShapeDtypeStruct((192, 384),...  159 us
    unnamed x16, local copies, waits for them, and re-layouts  9.33 us

profile of v3, /device:TPU:0, one launch (start us, length us, event | category | flops | bytes accessed | tf_op | source)
XLA Modules:
  0.0 178.0 jit_solution(192364823594520126)
XLA Ops:
  0.7 1.0 convert_reduce_fusion
  1.7 0.8 multiply_add_fusion.1
  2.4 0.0 copy-start.3
  2.4 0.5 copy-done.3
  2.9 0.7 select_reduce_fusion.4.home_local_ref
  3.6 0.7 broadcast_select_fusion
  4.3 0.6 select_reduce_fusion.2.own_slot_ref
  4.9 0.7 select_reduce_fusion.3.slot_lane_ref
  5.6 0.1 fusion.1
  5.7 0.6 convert_element_type.11.slot_live_ref
  6.3 0.8 constant_dynamic-slice_fusion
  7.1 0.1 copy.32.rows
  7.2 0.0 copy-start.2
  7.2 0.8 constant_dynamic-slice_fusion.1
  8.0 0.7 copy.31.s1_ref
  8.7 0.8 copy.26
  9.5 0.6 gather_fusion.1
  10.1 0.0 copy-start.1
  10.1 0.2 select_reduce_fusion
  10.3 0.1 copy.29
  10.4 0.1 copy.27
  10.5 0.6 broadcast_add_fusion
  11.1 0.0 copy-done.1
  11.1 0.0 copy-done.2
  11.1 0.8 copy.24
  11.9 1.2 gather_fusion
  13.1 158.6 %shard_map.120 = (bf16[192,384]{1,0:T(8,128)(2,1)}, bf16[192,384]{1,0:T(8,128)(2,1)}, bf16[12,15,16,128]{3,2,1,0:T(8,128)(2,1)}, bf16[18,15,16,128]{3,2,1,0:T(8,128)(2,1)}) custom-call(bf16[192,384]{1,0:T(8,128)(2,1)} %tok_ref.1, bf16[192,384]{1,0:T(8,128)(2,1)} %cot_ref.1, bf16[12,15,16,128]{3,2,1,0:T(8,128)(2,1)} %w1_ref.1, ...), custom_call_target="tpu_custom_call" | custom-call | tf_op jit(solution)/shard_map/pallas_call | solution.py:610
  171.7 0.0 copy-start
  171.7 1.7 copy.37
  173.4 1.6 copy.38
  174.9 2.1 %copy.39 = bf16[12,15,16,128]{3,2,1,0:T(8,128)(2,1)} copy(bf16[12,15,16,128]{3,2,1,0:T(8,128)(2,1)} %get-tuple-element.21) | data formatting | bytes 1474560
  177.0 0.0 copy-done
  177.0 1.0 copy.40
  (3 shorter events, 0.0 us)
Async XLA Ops:
  2.4 0.5 copy-start.3
  7.2 3.9 %copy-start.2 = (s32[12,15]{1,0:T(8,128)}, s32[12,15]{1,0:T(8,128)S(1)}, u32[]{:S(2)}) copy-start(s32[12,15]{1,0:T(8,128)S(1)} %copy.32.rows) | copy-start | bytes 2164
  10.1 1.0 copy-start.1
  171.7 5.4 %copy-start = (bf16[18,15,16,128]{3,2,1,0:T(8,128)(2,1)S(1)}, bf16[18,15,16,128]{3,2,1,0:T(8,128)(2,1)}, u32[]{:S(2)}) copy-start(bf16[18,15,16,128]{3,2,1,0:T(8,128)(2,1)} %get-tuple-element.22) | copy-start | bytes 3317764

commit v4 on v3

--- a/solution.py
+++ b/solution.py
@@ -337,11 +337,16 @@
             g2s[:, :, g, k] = gw2[:, k * 128 : (k + 1) * 128].reshape(4, 2, 16, 128)
         return 0
 
+    def flip(j, _):
+        xt[j] = xall[j].T
+        return 0
+
     lax.fori_loop(0, HALF, project, 0)
     grad_copy(0, 6).start()
     weights_last(1)
     lax.fori_loop(HALF, NB, project, 0)
     grad_copy(0, 7).start()
+    lax.fori_loop(0, 48, flip, 0)
 
     def pair_sum(w, chunk, h):
         own = grads[w]
@@ -446,18 +451,13 @@
 
         lax.fori_loop(0, 6, body, 0)
 
+    for i in (4, 7, 8, 9):
+        weight_copy(1, i).wait_recv()
+    mix((y + 2) % 4)
+    part_copy(0, 0, 2).start()
     pair_stage(0)
     pl.semaphore_signal(free_sem, inc=1, device_id=(sp, t), device_id_type=MESH)
-
-    def flip(j, _):
-        xt[j] = xall[j].T
-        return 0
-
-    lax.fori_loop(0, 48, flip, 0)
-    for i in (4, 7, 8, 9):
-        weight_copy(1, i).wait_recv()
-
-    for d in (2, 1, 3):
+    for d in (1, 3):
         mix((y + d) % 4)
         part_copy(0, 0, d).start()
 
@@ -467,41 +467,43 @@
         dact = lax.dot_general(dys, w2c, nt, preferred_element_type=F32).astype(BF)
         dpre = (dact.astype(F32) * slope[g]).astype(BF)
         dpre_all[:, pl.ds(pl.multiple_of(g * 128, 128), 128)] = dpre
+        return 0
+
+    def grad_one(g, _):
+        dpre = dpre_all[:, pl.ds(pl.multiple_of(g * 128, 128), 128)]
         for k in range(NK):
             gw1 = jnp.dot(xt[rows[g, k]], dpre, preferred_element_type=F32).astype(BF)
             g1s[:, :, g, k] = gw1.reshape(4, 2, 16, 128)
         return 0
 
-    lax.fori_loop(0, HALF, hidden, 0)
-    pl.semaphore_wait(free_sem, 1)
-    grad_copy(1, 6).start()
-    lax.fori_loop(HALF, NB, hidden, 0)
-    grad_copy(1, 7).start()
-    pass_stage(0)
-    pair_stage(1)
-    back((z + 2) % 4)
-    part_copy(1, 0, 2).start()
-
     def keep_two(g, k, value):
         g2s[x, c, g, k] = value
-
-    last_stage(0, keep_two, s2_ref)
-    lanes_sent(0)
 
     def lanes_back(i, _):
         s = home_local_ref[i]
         lanes[i // 16, (i // 4) % 4, i % 4] = g2s[x, c, s]
         return 0
 
-    lax.fori_loop(0, 32, lanes_back, 0)
-    lanes_go(1)
+    lax.fori_loop(0, NB, hidden, 0)
+    back((z + 2) % 4)
+    part_copy(1, 0, 2).start()
+    pass_stage(0)
     for d in (1, 3):
         back((z + d) % 4)
         part_copy(1, 0, d).start()
-    pass_stage(1)
+    lax.fori_loop(0, HALF, grad_one, 0)
+    pl.semaphore_wait(free_sem, 1)
+    grad_copy(1, 6).start()
+    last_stage(0, keep_two, s2_ref)
+    lanes_sent(0)
+    lax.fori_loop(0, 32, lanes_back, 0)
+    lanes_go(1)
+    lax.fori_loop(HALF, NB, grad_one, 0)
+    grad_copy(1, 7).start()
     mix(y)
+    pair_stage(1)
+    back(z)
     lanes_turn(1)
-    back(z)
     for w in range(2):
         for d in range(1, 4):
             part_copy(w, 0, d).wait_recv()
@@ -519,6 +521,7 @@
         lax.fori_loop(0, 12, add_four, 0)
         for d in range(1, 4):
             part_copy(w, 1, d).start()
+    pass_stage(1)
     for w, out in ((0, mixed), (1, dxo)):
         for d in range(1, 4):
             part_copy(w, 1, d).wait_recv()
@@ -585,6 +588,15 @@
     return home_lane, home_q, own_slot, home_local, slot_lane, slot_live
 
 
+def hand_over(*refs):
+    sem = refs[8]
+    copies = [pltpu.make_async_copy(refs[i], refs[4 + i], sem.at[i]) for i in range(4)]
+    for cp in copies:
+        cp.start()
+    for cp in copies:
+        cp.wait()
+
+
 VM = pl.BlockSpec(memory_space=pltpu.VMEM)
 SM = pl.BlockSpec(memory_space=pltpu.SMEM)
 ANY = pl.BlockSpec(memory_space=pl.ANY)
@@ -607,14 +619,15 @@
     scale_two = w2_scale[home_q]
     dma = pltpu.SemaphoreType.DMA
     part = (4, 4, 3, 192, 128)
-    return pl.pallas_call(
+    outs = [
+        jax.ShapeDtypeStruct((192, 384), BF),
+        jax.ShapeDtypeStruct((192, 384), BF),
+        jax.ShapeDtypeStruct(SHARD, BF),
+        jax.ShapeDtypeStruct((CAP, NK, 16, 128), BF),
+    ]
+    results = pl.pallas_call(
         layer_kernel,
-        out_shape=[
-            jax.ShapeDtypeStruct((192, 384), BF),
-            jax.ShapeDtypeStruct((192, 384), BF),
-            jax.ShapeDtypeStruct(SHARD, BF),
-            jax.ShapeDtypeStruct((CAP, NK, 16, 128), BF),
-        ],
+        out_shape=outs,
         in_specs=[ANY] * 4 + [SM] * 11,
         out_specs=[VM] * 4,
         scratch_shapes=[
@@ -674,6 +687,13 @@
         slot_lane,
         slot_live,
     )
+    return pl.pallas_call(
+        hand_over,
+        out_shape=outs,
+        in_specs=[ANY] * 4,
+        out_specs=[ANY] * 4,
+        scratch_shapes=[dma((4,))],
+    )(*results)
 
 
 def solution(mesh):

time: 179 us -> 228 us (1.27)
  Pallas kernels: 159 us -> 214 us
  local copies, waits for them, and re-layouts: 12.8 us -> 6.45 us
    pallas_call x1 -> x2, Pallas kernels: 159 us -> 214 us  [the longest x1 148 us: local(): pl.pallas_call(layer_kernel, out_shape=outs, in_specs=[ANY] * 4 + [SM] *...]
    unnamed x16 -> x10, local copies, waits for them, and re-layouts: 9.33 us -> 2.97 us
where the time goes in v4:
time: 228 us; the launch traced here: 227 us
  Pallas kernels  214 us (94%)
  local copies, waits for them, and re-layouts  6.45 us (3%)
  other arithmetic  5.95 us (3%)
    pallas_call x1, Pallas kernels, local(): pl.pallas_call(layer_kernel, out_shape=outs, in_specs=[ANY] * 4 + [SM] *...  148 us
    pallas_call x1, Pallas kernels, local(): pl.pallas_call(hand_over, out_shape=outs, in_specs=[ANY] * 4, out_specs=[...  65.9 us

profile of v4, /device:TPU:0, one launch (start us, length us, event | category | flops | bytes accessed | tf_op | source)
XLA Modules:
  0.0 226.7 jit_solution(6731027627448276768)
XLA Ops:
  0.7 1.0 convert_reduce_fusion
  1.7 0.8 multiply_add_fusion.1
  2.4 0.0 copy-start.2
  2.4 0.5 copy-done.2
  2.9 0.7 select_reduce_fusion.4.home_local_ref
  3.6 0.7 broadcast_select_fusion
  4.3 0.6 select_reduce_fusion.2.own_slot_ref
  4.9 0.7 select_reduce_fusion.3.slot_lane_ref
  5.6 0.1 fusion.1
  5.7 0.6 convert_element_type.11.slot_live_ref
  6.3 0.8 constant_dynamic-slice_fusion
  7.1 0.1 copy.32.rows
  7.2 0.0 copy-start.1
  7.2 0.8 constant_dynamic-slice_fusion.1
  8.0 0.7 copy.31.s1_ref
  8.7 0.8 copy.26
  9.5 0.6 gather_fusion.1
  10.1 0.0 copy-start
  10.1 0.2 select_reduce_fusion
  10.3 0.1 copy.29
  10.4 0.1 copy.27
  10.5 0.6 broadcast_add_fusion
  11.1 0.0 copy-done
  11.1 0.0 copy-done.1
  11.1 0.8 copy.24
  11.9 1.2 gather_fusion
  13.1 147.7 %shard_map.120 = (bf16[192,384]{1,0:T(8,128)(2,1)}, bf16[192,384]{1,0:T(8,128)(2,1)}, bf16[12,15,16,128]{3,2,1,0:T(8,128)(2,1)}, bf16[18,15,16,128]{3,2,1,0:T(8,128)(2,1)}) custom-call(bf16[192,384]{1,0:T(8,128)(2,1)} %tok_ref.1, bf16[192,384]{1,0:T(8,128)(2,1)} %cot_ref.1, bf16[12,15,16,128]{3,2,1,0:T(8,128)(2,1)} %w1_ref.1, ...), custom_call_target="tpu_custom_call" | custom-call | tf_op jit(solution)/shard_map/pallas_call | solution.py:628
  160.8 65.9 %shard_map.121 = (bf16[192,384]{1,0:T(8,128)(2,1)}, bf16[192,384]{1,0:T(8,128)(2,1)}, bf16[12,15,16,128]{3,2,1,0:T(8,128)(2,1)}, bf16[18,15,16,128]{3,2,1,0:T(8,128)(2,1)}) custom-call(bf16[192,384]{1,0:T(8,128)(2,1)} %get-tuple-element.8.refs_0_, bf16[192,384]{1,0:T(8,128)(2,1)} %get-tuple-element.9.refs_1_, ...), custom_call_target="tpu_custom_call" | custom-call | tf_op jit(solution)/shard_map/pallas_call | solution.py:690
  (3 shorter events, 0.0 us)
Async XLA Ops:
  2.4 0.5 copy-start.2
  7.2 3.9 %copy-start.1 = (s32[12,15]{1,0:T(8,128)}, s32[12,15]{1,0:T(8,128)S(1)}, u32[]{:S(2)}) copy-start(s32[12,15]{1,0:T(8,128)S(1)} %copy.32.rows) | copy-start | bytes 2164
  10.1 1.0 copy-start

commit v5 on v4

--- a/solution.py
+++ b/solution.py
@@ -39,15 +39,10 @@
     w2_ref,
     s1_ref,
     s2_ref,
-    rows,
-    cols,
-    kv1,
-    kv2,
-    own_slot_ref,
-    home_lane_ref,
-    home_local_ref,
-    slot_lane_ref,
-    slot_live_ref,
+    rows_ref,
+    cols_ref,
+    tab,
+    kv_ref,
     mixed,
     dxo,
     o1,
@@ -102,6 +97,18 @@
     landed = (rbuf, rback)
     nt = (((1,), (1,)), ((), ()))
 
+    def row(g, k):
+        return rows_ref[k, t * NB + g]
+
+    def col(g, k):
+        return cols_ref[k, tab[HOME_Q + g]]
+
+    def scale1(g, k):
+        return s1_ref[k, t * NB + g]
+
+    def scale2(g, k):
+        return s2_ref[k, tab[HOME_Q + g]]
+
     def lane_copy(trip, j, step, d):
         along_y = (j == 0) == (step == 0)
         peer_y, peer_z = ((y + d) % 4, z) if along_y else (y, (z + d) % 4)
@@ -235,7 +242,7 @@
     loads[0].wait()
 
     def lanes_out(i, _):
-        s = own_slot_ref[i]
+        s = tab[OWN_SLOT + i]
         lanes[i // 16, (i // 4) % 4, i % 4] = w2in[s]
         return 0
 
@@ -246,7 +253,7 @@
 
     def scale_one(g, _):
         for k in range(NK):
-            w1all[p, g, k] = (w1in[g, k].astype(F32) * s1_ref[g, k]).astype(BF)
+            w1all[p, g, k] = (w1in[g, k].astype(F32) * scale1(g, k)).astype(BF)
         return 0
 
     lax.fori_loop(0, NB, scale_one, 0)
@@ -281,9 +288,9 @@
     lanes_end(0)
 
     def scale_two(g, _):
-        i = home_lane_ref[g]
+        i = tab[HOME_LANE + g]
         for k in range(NK):
-            w2all[p, g, k] = (rbuf[i // 16, (i // 4) % 4, i % 4, k].astype(F32) * s2_ref[g, k]).astype(BF)
+            w2all[p, g, k] = (rbuf[i // 16, (i // 4) % 4, i % 4, k].astype(F32) * scale2(g, k)).astype(BF)
         return 0
 
     lax.fori_loop(0, NB, scale_two, 0)
@@ -323,7 +330,7 @@
 
     def project(g, _):
         w1c = jnp.concatenate([w1all[:, g, k].reshape(128, 128) for k in range(NK)], axis=0)
-        xs = jnp.concatenate([xall[rows[g, k]] for k in range(NK)], axis=1)
+        xs = jnp.concatenate([xall[row(g, k)] for k in range(NK)], axis=1)
         pre = jnp.dot(xs, w1c, preferred_element_type=F32)
         th = jnp.tanh(GELU_C * (pre + GELU_A * pre * pre * pre))
         act = (0.5 * pre * (1.0 + th)).astype(BF)
@@ -331,7 +338,7 @@
             1.0 + 3.0 * GELU_A * pre * pre
         )
         act_all[:, pl.ds(pl.multiple_of(g * 128, 128), 128)] = act
-        dys = jnp.concatenate([dyall[cols[g, k]] for k in range(NK)], axis=1)
+        dys = jnp.concatenate([dyall[col(g, k)] for k in range(NK)], axis=1)
         gw2 = jnp.dot(act.T, dys, preferred_element_type=F32).astype(BF)
         for k in range(NK):
             g2s[:, :, g, k] = gw2[:, k * 128 : (k + 1) * 128].reshape(4, 2, 16, 128)
@@ -403,18 +410,18 @@
             for k in range(NK):
                 total = own[x, c, g, k].astype(F32) + fin[w, 0, g, k].astype(F32)
                 total = total + fin[w, 1, g, k].astype(F32)
-                out(g, k, (total * scale[g, k]).astype(BF))
+                out(g, k, (total * scale(g, k)).astype(BF))
             return 0
 
         lax.fori_loop(0, NB, body, 0)
 
-    def mix(row):
+    def mix(to_y):
         def body(i, _):
-            j = 12 * row + 2 * i
+            j = 12 * to_y + 2 * i
             panel = jnp.concatenate(
                 [
                     jnp.concatenate(
-                        [w2all[:, g, kv2[j + b, g]].reshape(128, 128) for g in range(NB)], axis=0
+                        [w2all[:, g, kv_ref[NB + g, j + b]].reshape(128, 128) for g in range(NB)], axis=0
                     )
                     for b in range(2)
                 ],
@@ -423,19 +430,19 @@
             res = jnp.dot(act_all[...], panel, preferred_element_type=F32).astype(BF)
             for b in range(2):
                 at = 2 * i + b
-                m_part[row, at // 3, at % 3] = res[:, b * 128 : (b + 1) * 128]
+                m_part[to_y, at // 3, at % 3] = res[:, b * 128 : (b + 1) * 128]
             return 0
 
         lax.fori_loop(0, 6, body, 0)
 
-    def back(col):
+    def back(to_z):
         def body(i, _):
             at = (2 * i, 2 * i + 1)
             panel = jnp.concatenate(
                 [
                     jnp.concatenate(
                         [
-                            w1all[:, g, kv1[12 * (a // 3) + 3 * col + a % 3, g]].reshape(128, 128)
+                            w1all[:, g, kv_ref[g, 12 * (a // 3) + 3 * to_z + a % 3]].reshape(128, 128)
                             for g in range(NB)
                         ],
                         axis=1,
@@ -446,7 +453,7 @@
             )
             res = lax.dot_general(dpre_all[...], panel, nt, preferred_element_type=F32).astype(BF)
             for b, a in enumerate(at):
-                d_part[a // 3, col, a % 3] = res[:, b * 128 : (b + 1) * 128]
+                d_part[a // 3, to_z, a % 3] = res[:, b * 128 : (b + 1) * 128]
             return 0
 
         lax.fori_loop(0, 6, body, 0)
@@ -463,7 +470,7 @@
 
     def hidden(g, _):
         w2c = jnp.concatenate([w2all[:, g, k].reshape(128, 128) for k in range(NK)], axis=1)
-        dys = jnp.concatenate([dyall[cols[g, k]] for k in range(NK)], axis=1)
+        dys = jnp.concatenate([dyall[col(g, k)] for k in range(NK)], axis=1)
         dact = lax.dot_general(dys, w2c, nt, preferred_element_type=F32).astype(BF)
         dpre = (dact.astype(F32) * slope[g]).astype(BF)
         dpre_all[:, pl.ds(pl.multiple_of(g * 128, 128), 128)] = dpre
@@ -472,7 +479,7 @@
     def grad_one(g, _):
         dpre = dpre_all[:, pl.ds(pl.multiple_of(g * 128, 128), 128)]
         for k in range(NK):
-            gw1 = jnp.dot(xt[rows[g, k]], dpre, preferred_element_type=F32).astype(BF)
+            gw1 = jnp.dot(xt[row(g, k)], dpre, preferred_element_type=F32).astype(BF)
             g1s[:, :, g, k] = gw1.reshape(4, 2, 16, 128)
         return 0
 
@@ -480,7 +487,7 @@
         g2s[x, c, g, k] = value
 
     def lanes_back(i, _):
-        s = home_local_ref[i]
+        s = tab[HOME_LOCAL + i]
         lanes[i // 16, (i // 4) % 4, i % 4] = g2s[x, c, s]
         return 0
 
@@ -494,7 +501,7 @@
     lax.fori_loop(0, HALF, grad_one, 0)
     pl.semaphore_wait(free_sem, 1)
     grad_copy(1, 6).start()
-    last_stage(0, keep_two, s2_ref)
+    last_stage(0, keep_two, scale2)
     lanes_sent(0)
     lax.fori_loop(0, 32, lanes_back, 0)
     lanes_go(1)
@@ -533,9 +540,9 @@
     lanes_end(1)
 
     def slot_out(s, _):
-        i = slot_lane_ref[s]
+        i = tab[SLOT_LANE + s]
         got = rback[i // 16, (i // 4) % 4, i % 4]
-        o2[s] = jnp.where(slot_live_ref[s] > 0, got, jnp.zeros_like(got))
+        o2[s] = jnp.where(s < tab[SLOTS_HERE], got, jnp.zeros_like(got))
         return 0
 
     lax.fori_loop(0, CAP, slot_out, 0)
@@ -543,7 +550,7 @@
     def keep_one(g, k, value):
         o1[g, k] = value
 
-    last_stage(1, keep_one, s1_ref)
+    last_stage(1, keep_one, scale1)
     lanes_sent(1)
     for w in range(2):
         for i in range(10):
@@ -558,42 +565,65 @@
                 part_copy(w, step, d).wait_send()
 
 
-def route_tables(owner, rank):
-    index = jnp.arange(192, dtype=jnp.int32)
-    source = index // NB
-    earlier = index[None, :] < index[:, None]
-    same_dest = owner[None, :] == owner[:, None]
-    same_src = source[None, :] == source[:, None]
-    slot = jnp.sum((earlier & same_dest).astype(jnp.int32), axis=1)
-    pair = jnp.sum((earlier & same_dest & same_src).astype(jnp.int32), axis=1)
-    mine_first = rank * NB
-    mine_owner = lax.dynamic_slice(owner, (mine_first,), (NB,))
-    mine_pair = lax.dynamic_slice(pair, (mine_first,), (NB,))
-    mine_slot = lax.dynamic_slice(slot, (mine_first,), (NB,))
-    home_lane = mine_pair * 16 + mine_owner
-    home_q = mine_owner * CAP + mine_slot
-    lane = jnp.arange(32, dtype=jnp.int32)
-    mine_lane = jnp.where(owner == rank, pair * 16 + source, -1)
-    own_slot = jnp.sum(jnp.where(lane[:, None] == mine_lane[None, :], slot[None, :], 0), axis=1)
-    home_local = jnp.sum(
-        jnp.where(
-            lane[:, None] == home_lane[None, :], jnp.arange(NB, dtype=jnp.int32)[None, :], 0
-        ),
-        axis=1,
-    )
-    mine_at = jnp.where(owner == rank, slot, -1)
-    hit = jnp.arange(CAP, dtype=jnp.int32)[:, None] == mine_at[None, :]
-    slot_lane = jnp.sum(jnp.where(hit, (pair * 16 + source)[None, :], 0), axis=1)
-    slot_live = jnp.any(hit, axis=1).astype(jnp.int32)
-    return home_lane, home_q, own_slot, home_local, slot_lane, slot_live
+OWN_SLOT, HOME_LOCAL, HOME_LANE, HOME_Q, SLOT_LANE, SLOTS_HERE, SPARE = 0, 32, 64, 80, 96, 120, 128
+
+
+def table_kernel(owner, rows, cols, tab, kv, count, pairs):
+    t = lax.axis_index("tensor")
+    for i in range(16):
+        count[i] = 0
+    for i in range(32):
+        tab[OWN_SLOT + i] = 0
+        tab[HOME_LOCAL + i] = 0
+    for s in range(CAP):
+        tab[SLOT_LANE + s] = 0
+
+    def source(src, _):
+        for i in range(16):
+            pairs[i] = 0
+        for i in range(NB):
+            o = owner[src * NB + i]
+            slot, pair = count[o], pairs[o]
+            count[o] = slot + 1
+            pairs[o] = pair + 1
+            here = o == t
+            tab[jnp.where(here, OWN_SLOT + pair * 16 + src, SPARE)] = slot
+            tab[jnp.where(here, SLOT_LANE + slot, SPARE + 1)] = pair * 16 + src
+
+            @pl.when(src == t)
+            def _():
+                tab[HOME_LANE + i] = pair * 16 + o
+                tab[HOME_Q + i] = o * CAP + slot
+                tab[HOME_LOCAL + pair * 16 + o] = i
+
+        return 0
+
+    lax.fori_loop(0, 16, source, 0)
+    tab[SLOTS_HERE] = count[t]
+
+    def inverse(g, _):
+        for j in range(48):
+            kv[g, j] = NK
+            kv[NB + g, j] = NK
+        q = tab[HOME_Q + g]
+        for k in range(NK):
+            kv[g, rows[k, t * NB + g]] = k
+            kv[NB + g, cols[k, q]] = k
+        return 0
+
+    lax.fori_loop(0, NB, inverse, 0)
 
 
 def hand_over(*refs):
-    sem = refs[8]
-    copies = [pltpu.make_async_copy(refs[i], refs[4 + i], sem.at[i]) for i in range(4)]
-    for cp in copies:
-        cp.start()
-    for cp in copies:
+    src, dst, kept, sem = refs[:4], refs[4:8], refs[8:12], refs[12]
+    loads = [pltpu.make_async_copy(src[i], kept[i], sem.at[0, i]) for i in range(4)]
+    stores = [pltpu.make_async_copy(kept[i], dst[i], sem.at[1, i]) for i in range(4)]
+    for i in (3, 2, 0, 1):
+        loads[i].start()
+    for i in (3, 2, 0, 1):
+        loads[i].wait()
+        stores[i].start()
+    for cp in stores:
         cp.wait()
 
 
@@ -604,19 +634,7 @@
 LANES = (2, 4, 4, NK, 16, 128)
 
 
-def inverse(index):
-    k = jnp.arange(NK, dtype=jnp.int32)
-    hit = index[None, :, :] == jnp.arange(48, dtype=jnp.int32)[:, None, None]
-    return NK + jnp.sum(jnp.where(hit, k[None, None, :] - NK, 0), axis=2)
-
-
 def local(tokens, cotangent, w1_blocks, w1_rows, w1_scale, w2_blocks, w2_cols, w2_scale, owner):
-    rank = lax.axis_index("tensor")
-    home_lane, home_q, own_slot, home_local, slot_lane, slot_live = route_tables(owner, rank)
-    rows = lax.dynamic_slice(w1_rows, (rank * NB, 0), (NB, NK))
-    scale_one = lax.dynamic_slice(w1_scale, (rank * NB, 0), (NB, NK))
-    cols = w2_cols[home_q]
-    scale_two = w2_scale[home_q]
     dma = pltpu.SemaphoreType.DMA
     part = (4, 4, 3, 192, 128)
     outs = [
@@ -625,10 +643,20 @@
         jax.ShapeDtypeStruct(SHARD, BF),
         jax.ShapeDtypeStruct((CAP, NK, 16, 128), BF),
     ]
+    tab, kv = pl.pallas_call(
+        table_kernel,
+        out_shape=[
+            jax.ShapeDtypeStruct((256,), jnp.int32),
+            jax.ShapeDtypeStruct((2 * NB, 48), jnp.int32),
+        ],
+        in_specs=[SM] * 3,
+        out_specs=[SM] * 2,
+        scratch_shapes=[pltpu.SMEM((16,), jnp.int32), pltpu.SMEM((16,), jnp.int32)],
+    )(owner, w1_rows.T, w2_cols.T)
     results = pl.pallas_call(
         layer_kernel,
         out_shape=outs,
-        in_specs=[ANY] * 4 + [SM] * 11,
+        in_specs=[ANY] * 4 + [SM] * 6,
         out_specs=[VM] * 4,
         scratch_shapes=[
             pltpu.VMEM(SHARD, BF),
@@ -675,24 +703,19 @@
         cotangent,
         w1_blocks,
         w2_blocks,
-        scale_one,
-        scale_two,
-        rows,
-        cols,
-        inverse(rows),
-        inverse(cols),
-        own_slot,
-        home_lane,
-        home_local,
-        slot_lane,
-        slot_live,
+        w1_scale.T,
+        w2_scale.T,
+        w1_rows.T,
+        w2_cols.T,
+        tab,
+        kv,
     )
     return pl.pallas_call(
         hand_over,
         out_shape=outs,
         in_specs=[ANY] * 4,
         out_specs=[ANY] * 4,
-        scratch_shapes=[dma((4,))],
+        scratch_shapes=[pltpu.VMEM(o.shape, BF) for o in outs] + [dma((2, 4))],
     )(*results)
 
 

time: 228 us -> 158 us (0.69)
  Pallas kernels: 214 us -> 157 us
  local copies, waits for them, and re-layouts: 6.45 us -> 0 us
  other arithmetic: 5.95 us -> 0 us
    pallas_call x1, Pallas kernels: 65.9 us -> 2.63 us  [local(): pl.pallas_call(hand_over, out_shape=outs, in_specs=[ANY] * 4, out_specs=[...]
    pallas_call x0 -> x1, Pallas kernels: none -> 5.83 us  [local(): pl.pallas_call(table_kernel, out_shape=[jax.ShapeDtypeStruct((256,), jnp....]
    reduce_sum x5 -> x0, other arithmetic: 3.15 us -> none  [the longest x1 1 us: route_tables(): pair = jnp.sum((earlier & same_dest & same_src).astype(jnp.int32), axis=1)]
    unnamed x10 -> x0, local copies, waits for them, and re-layouts: 2.97 us -> none
where the time goes in v5:
time: 158 us; the launch traced here: 157 us
  Pallas kernels  157 us (99%)
    pallas_call x1, Pallas kernels, local(): pl.pallas_call(layer_kernel, out_shape=outs, in_specs=[ANY] * 4 + [SM] *...  148 us
    pallas_call x1, Pallas kernels, local(): pl.pallas_call(table_kernel, out_shape=[jax.ShapeDtypeStruct((256,), jnp....  5.83 us

profile of v5, /device:TPU:0, one launch (start us, length us, event | category | flops | bytes accessed | tf_op | source)
XLA Modules:
  0.0 157.3 jit_solution(4973430725497780086)
XLA Ops:
  0.6 5.8 %shard_map.120 = (s32[256]{0:T(256)}, s32[24,48]{1,0:T(8,128)}) custom-call(s32[192]{0:T(256)} %owner.1, s32[15,192]{1,0:T(8,128)} %bitcast.6, s32[15,288]{1,0:T(8,128)} %bitcast.4), custom_call_target="tpu_custom_call" | custom-call | tf_op jit(solution)/shard_map/pallas_call | solution.py:646
  6.5 148.2 %shard_map.121 = (bf16[192,384]{1,0:T(8,128)(2,1)}, bf16[192,384]{1,0:T(8,128)(2,1)}, bf16[12,15,16,128]{3,2,1,0:T(8,128)(2,1)}, bf16[18,15,16,128]{3,2,1,0:T(8,128)(2,1)}) custom-call(bf16[192,384]{1,0:T(8,128)(2,1)} %tok_ref.1, bf16[192,384]{1,0:T(8,128)(2,1)} %cot_ref.1, bf16[12,15,16,128]{3,2,1,0:T(8,128)(2,1)} %w1_ref.1, ...), custom_call_target="tpu_custom_call" | custom-call | tf_op jit(solution)/shard_map/pallas_call | solution.py:656
  154.7 2.6 %shard_map.122 = (bf16[192,384]{1,0:T(8,128)(2,1)}, bf16[192,384]{1,0:T(8,128)(2,1)}, bf16[12,15,16,128]{3,2,1,0:T(8,128)(2,1)}, bf16[18,15,16,128]{3,2,1,0:T(8,128)(2,1)}) custom-call(bf16[192,384]{1,0:T(8,128)(2,1)} %get-tuple-element.12.refs_0_, bf16[192,384]{1,0:T(8,128)(2,1)} %get-tuple-element.13.refs_1_, ...), custom_call_target="tpu_custom_call" | custom-call | tf_op jit(solution)/shard_map/pallas_call | solution.py:713

commit v6 on v5

--- a/solution.py
+++ b/solution.py
@@ -69,6 +69,7 @@
     m_part,
     d_part,
     f_buf,
+    f_hop,
     f_fin,
     a_send,
     a_recv,
@@ -109,46 +110,50 @@
     def scale2(g, k):
         return s2_ref[k, tab[HOME_Q + g]]
 
-    def lane_copy(trip, j, step, d):
+    def lane_copy(trip, j, step, d, piece):
         along_y = (j == 0) == (step == 0)
         peer_y, peer_z = ((y + d) % 4, z) if along_y else (y, (z + d) % 4)
+        ks = (pl.ds(0, 8), pl.ds(8, NK - 8))[piece]
         src = lanes.at[j] if step == 0 else middle.at[trip, j]
         dst = middle.at[trip, j] if step == 0 else landed[trip].at[j]
         return pltpu.make_async_remote_copy(
-            src.at[peer_y] if along_y else src.at[:, peer_z],
-            dst.at[y] if along_y else dst.at[:, z],
-            a_send.at[trip, j, step, d],
-            a_recv.at[trip, j, step, d],
+            src.at[peer_y, :, ks] if along_y else src.at[:, peer_z, ks],
+            dst.at[y, :, ks] if along_y else dst.at[:, z, ks],
+            a_send.at[trip, j, step, d, piece],
+            a_recv.at[trip, j, step, d, piece],
             device_id=(p, peer_y * 4 + peer_z),
             device_id_type=MESH,
         )
 
     def lanes_go(trip):
-        for d in (2, 1, 3):
-            for j in range(2):
-                lane_copy(trip, j, 0, d).start()
+        for piece in range(2):
+            for d in (2, 1, 3):
+                for j in range(2):
+                    lane_copy(trip, j, 0, d, piece).start()
         middle[trip, 0, y] = lanes[0, y]
         middle[trip, 1, :, z] = lanes[1, :, z]
 
-    def lanes_turn(trip):
+    def lanes_turn(trip, piece):
         for j in range(2):
             for d in range(1, 4):
-                lane_copy(trip, j, 0, d).wait_recv()
+                lane_copy(trip, j, 0, d, piece).wait_recv()
             for d in (2, 1, 3):
-                lane_copy(trip, j, 1, d).start()
+                lane_copy(trip, j, 1, d, piece).start()
+
+    def lanes_end(trip):
         landed[trip][0, :, z] = middle[trip, 0, :, z]
         landed[trip][1, y] = middle[trip, 1, y]
-
-    def lanes_end(trip):
-        for j in range(2):
-            for d in range(1, 4):
-                lane_copy(trip, j, 1, d).wait_recv()
+        for piece in range(2):
+            for j in range(2):
+                for d in range(1, 4):
+                    lane_copy(trip, j, 1, d, piece).wait_recv()
 
     def lanes_sent(trip):
         for j in range(2):
             for step in range(2):
                 for d in range(1, 4):
-                    lane_copy(trip, j, step, d).wait_send()
+                    for piece in range(2):
+                        lane_copy(trip, j, step, d, piece).wait_send()
 
     def weight_copy(w, i):
         who, part, dev = (
@@ -206,13 +211,26 @@
             src, dst, g_send.at[w, i], g_recv.at[w, i], device_id=(dev, t), device_id_type=MESH
         )
 
+    def shards_of(w, place, lo, n):
+        return (place, pl.ds(lo, n)) if w == 0 else (pl.ds(lo, n), place)
+
     def part_copy(w, step, d):
         along_y = (w == 0) == (step == 0)
-        peer_y, peer_z = ((y + d) % 4, z) if along_y else (y, (z + d) % 4)
         if step == 0:
-            src = parts[w].at[peer_y] if along_y else parts[w].at[:, peer_z]
-            dst = f_buf.at[w, d - 1]
+            here = y if w == 0 else z
+            up, down, far = (here + 1) % 4, (here + 3) % 4, (here + 2) % 4
+            place, lo, dst, to = (
+                (far, 0, f_hop.at[w, 0], 1),
+                (far, 2, f_hop.at[w, 1], 3),
+                (up, 2, f_buf.at[w, 0, pl.ds(2, 2)], 1),
+                (down, 0, f_buf.at[w, 1, pl.ds(0, 2)], 3),
+                (up, 0, f_buf.at[w, 0, pl.ds(0, 2)], 1),
+                (down, 2, f_buf.at[w, 1, pl.ds(2, 2)], 3),
+            )[d]
+            src = parts[w].at[shards_of(w, place, lo, 2)]
+            peer_y, peer_z = ((y + to) % 4, z) if along_y else (y, (z + to) % 4)
         else:
+            peer_y, peer_z = ((y + d) % 4, z) if along_y else (y, (z + d) % 4)
             src = parts[w].at[peer_y, peer_z]
             dst = f_fin.at[w, d - 1]
         return pltpu.make_async_remote_copy(
@@ -223,6 +241,22 @@
             device_id=(p, peer_y * 4 + peer_z),
             device_id_type=MESH,
         )
+
+    def part_on(w, way):
+        here = y if w == 0 else z
+        place = (here + (1, 3)[way]) % 4
+        part = parts[w]
+        part_copy(w, 0, way).wait_recv()
+
+        def add(i, _):
+            a, b = i // 3 + 2 * way, i % 3
+            at = (place, a) if w == 0 else (a, place)
+            total = part[at[0], at[1], b].astype(F32) + f_hop[w, way, i // 3, b].astype(F32)
+            part[at[0], at[1], b] = total.astype(BF)
+            return 0
+
+        lax.fori_loop(0, 6, add, 0)
+        part_copy(w, 0, 4 + way).start()
 
     loads = [
         pltpu.make_async_copy(w2_ref, w2in, l_sem.at[0]),
@@ -279,7 +313,8 @@
         weight_copy(w, 6).wait_recv()
         weight_copy(w, 9).start()
 
-    lanes_turn(0)
+    lanes_turn(0, 0)
+    lanes_turn(0, 1)
     for group in (0, 1):
         for w in range(2):
             for i in range(2):
@@ -461,13 +496,10 @@
     for i in (4, 7, 8, 9):
         weight_copy(1, i).wait_recv()
     mix((y + 2) % 4)
-    part_copy(0, 0, 2).start()
+    part_copy(0, 0, 0).start()
+    part_copy(0, 0, 1).start()
     pair_stage(0)
     pl.semaphore_signal(free_sem, inc=1, device_id=(sp, t), device_id_type=MESH)
-    for d in (1, 3):
-        mix((y + d) % 4)
-        part_copy(0, 0, d).start()
-
     def hidden(g, _):
         w2c = jnp.concatenate([w2all[:, g, k].reshape(128, 128) for k in range(NK)], axis=1)
         dys = jnp.concatenate([dyall[col(g, k)] for k in range(NK)], axis=1)
@@ -491,28 +523,42 @@
         lanes[i // 16, (i // 4) % 4, i % 4] = g2s[x, c, s]
         return 0
 
+    def mix_go(way):
+        mix((y + (1, 3)[way]) % 4)
+        part_copy(0, 0, 2 + way).start()
+        part_on(0, way)
+
+    def back_go(way):
+        back((z + (1, 3)[way]) % 4)
+        part_copy(1, 0, 2 + way).start()
+        part_on(1, way)
+
     lax.fori_loop(0, NB, hidden, 0)
     back((z + 2) % 4)
-    part_copy(1, 0, 2).start()
-    pass_stage(0)
-    for d in (1, 3):
-        back((z + d) % 4)
-        part_copy(1, 0, d).start()
+    part_copy(1, 0, 0).start()
+    part_copy(1, 0, 1).start()
+    mix_go(0)
     lax.fori_loop(0, HALF, grad_one, 0)
     pl.semaphore_wait(free_sem, 1)
     grad_copy(1, 6).start()
+    pass_stage(0)
+    mix_go(1)
+    back_go(0)
+    lax.fori_loop(HALF, NB, grad_one, 0)
+    grad_copy(1, 7).start()
+    back_go(1)
+    mix(y)
+    pair_stage(1)
     last_stage(0, keep_two, scale2)
     lanes_sent(0)
     lax.fori_loop(0, 32, lanes_back, 0)
     lanes_go(1)
-    lax.fori_loop(HALF, NB, grad_one, 0)
-    grad_copy(1, 7).start()
-    mix(y)
-    pair_stage(1)
     back(z)
-    lanes_turn(1)
+    lanes_turn(1, 0)
+    lanes_turn(1, 1)
+    pass_stage(1)
     for w in range(2):
-        for d in range(1, 4):
+        for d in range(2, 6):
             part_copy(w, 0, d).wait_recv()
         part = parts[w]
 
@@ -520,7 +566,7 @@
             a, b = i // 3, i % 3
             here = (y, a) if w == 0 else (a, z)
             total = part[here[0], here[1], b].astype(F32)
-            for d in range(3):
+            for d in range(2):
                 total = total + f_buf[w, d, a, b].astype(F32)
             part[here[0], here[1], b] = total.astype(BF)
             return 0
@@ -528,7 +574,6 @@
         lax.fori_loop(0, 12, add_four, 0)
         for d in range(1, 4):
             part_copy(w, 1, d).start()
-    pass_stage(1)
     for w, out in ((0, mixed), (1, dxo)):
         for d in range(1, 4):
             part_copy(w, 1, d).wait_recv()
@@ -560,9 +605,10 @@
                 feature_copy(w, group, i).wait_send()
         for i in range(8):
             grad_copy(w, i).wait_send()
-        for step in range(2):
-            for d in range(1, 4):
-                part_copy(w, step, d).wait_send()
+        for d in range(6):
+            part_copy(w, 0, d).wait_send()
+        for d in range(1, 4):
+            part_copy(w, 1, d).wait_send()
 
 
 OWN_SLOT, HOME_LOCAL, HOME_LANE, HOME_Q, SLOT_LANE, SLOTS_HERE, SPARE = 0, 32, 64, 80, 96, 120, 128
@@ -579,6 +625,7 @@
         tab[SLOT_LANE + s] = 0
 
     def source(src, _):
+        seen = []
         for i in range(16):
             pairs[i] = 0
         for i in range(NB):
@@ -590,8 +637,11 @@
             tab[jnp.where(here, OWN_SLOT + pair * 16 + src, SPARE)] = slot
             tab[jnp.where(here, SLOT_LANE + slot, SPARE + 1)] = pair * 16 + src
 
-            @pl.when(src == t)
-            def _():
+            seen.append((o, slot, pair))
+
+        @pl.when(src == t)
+        def _():
+            for i, (o, slot, pair) in enumerate(seen):
                 tab[HOME_LANE + i] = pair * 16 + o
                 tab[HOME_Q + i] = o * CAP + slot
                 tab[HOME_LOCAL + pair * 16 + o] = i
@@ -680,18 +730,19 @@
             pltpu.VMEM((2, 2) + SHARD, BF),
             pltpu.VMEM(part, BF),
             pltpu.VMEM(part, BF),
-            pltpu.VMEM((2, 3, 4, 3, 192, 128), BF),
+            pltpu.VMEM((2, 2, 4, 3, 192, 128), BF),
+            pltpu.VMEM((2, 2, 2, 3, 192, 128), BF),
             pltpu.VMEM((2, 3, 3, 192, 128), BF),
-            dma((2, 2, 2, 4)),
-            dma((2, 2, 2, 4)),
+            dma((2, 2, 2, 4, 2)),
+            dma((2, 2, 2, 4, 2)),
             dma((2, 10)),
             dma((2, 10)),
             dma((2, 5, 4)),
             dma((2, 5, 4)),
             dma((2, 8)),
             dma((2, 8)),
-            dma((2, 2, 4)),
-            dma((2, 2, 4)),
+            dma((2, 2, 6)),
+            dma((2, 2, 6)),
             dma((8,)),
             pltpu.SemaphoreType.REGULAR,
         ],

time: 158 us -> 152 us (0.962)
  Pallas kernels: 157 us -> 151 us
    pallas_call x1, Pallas kernels: 148 us -> 143 us  [local(): pl.pallas_call(layer_kernel, out_shape=outs, in_specs=[ANY] * 4 + [SM] *...]
where the time goes in v6:
time: 152 us
  Pallas kernels  151 us (99%)
    pallas_call x1, Pallas kernels, local(): pl.pallas_call(layer_kernel, out_shape=outs, in_specs=[ANY] * 4 + [SM] *...  143 us
    pallas_call x1, Pallas kernels, local(): pl.pallas_call(table_kernel, out_shape=[jax.ShapeDtypeStruct((256,), jnp....  5.8 us

profile of v6, /device:TPU:0, one launch (start us, length us, event | category | flops | bytes accessed | tf_op | source)
XLA Modules:
  0.0 151.6 jit_solution(898491577138924291)
XLA Ops:
  0.6 5.8 %shard_map.120 = (s32[256]{0:T(256)}, s32[24,48]{1,0:T(8,128)}) custom-call(s32[192]{0:T(256)} %owner.1, s32[15,192]{1,0:T(8,128)} %bitcast.6, s32[15,288]{1,0:T(8,128)} %bitcast.4), custom_call_target="tpu_custom_call" | custom-call | tf_op jit(solution)/shard_map/pallas_call | solution.py:696
  6.4 142.5 %shard_map.121 = (bf16[192,384]{1,0:T(8,128)(2,1)}, bf16[192,384]{1,0:T(8,128)(2,1)}, bf16[12,15,16,128]{3,2,1,0:T(8,128)(2,1)}, bf16[18,15,16,128]{3,2,1,0:T(8,128)(2,1)}) custom-call(bf16[192,384]{1,0:T(8,128)(2,1)} %tok_ref.1, bf16[192,384]{1,0:T(8,128)(2,1)} %cot_ref.1, bf16[12,15,16,128]{3,2,1,0:T(8,128)(2,1)} %w1_ref.1, ...), custom_call_target="tpu_custom_call" | custom-call | tf_op jit(solution)/shard_map/pallas_call | solution.py:706
  148.9 2.6 %shard_map.122 = (bf16[192,384]{1,0:T(8,128)(2,1)}, bf16[192,384]{1,0:T(8,128)(2,1)}, bf16[12,15,16,128]{3,2,1,0:T(8,128)(2,1)}, bf16[18,15,16,128]{3,2,1,0:T(8,128)(2,1)}) custom-call(bf16[192,384]{1,0:T(8,128)(2,1)} %get-tuple-element.12.refs_0_, bf16[192,384]{1,0:T(8,128)(2,1)} %get-tuple-element.13.refs_1_, ...), custom_call_target="tpu_custom_call" | custom-call | tf_op jit(solution)/shard_map/pallas_call | solution.py:764

commit v7 on v6

--- a/solution.py
+++ b/solution.py
@@ -533,6 +533,23 @@
         part_copy(1, 0, 2 + way).start()
         part_on(1, way)
 
+    def part_turn(w):
+        for d in range(2, 6):
+            part_copy(w, 0, d).wait_recv()
+        part = parts[w]
+
+        def add_four(i, _):
+            a, b = i // 3, i % 3
+            here = (y, a) if w == 0 else (a, z)
+            total = part[here[0], here[1], b].astype(F32)
+            for d in range(2):
+                total = total + f_buf[w, d, a, b].astype(F32)
+            part[here[0], here[1], b] = total.astype(BF)
+            return 0
+
+        lax.fori_loop(0, 12, add_four, 0)
+        for d in range(1, 4):
+            part_copy(w, 1, d).start()
     lax.fori_loop(0, NB, hidden, 0)
     back((z + 2) % 4)
     part_copy(1, 0, 0).start()
@@ -546,34 +563,19 @@
     back_go(0)
     lax.fori_loop(HALF, NB, grad_one, 0)
     grad_copy(1, 7).start()
-    back_go(1)
-    mix(y)
-    pair_stage(1)
     last_stage(0, keep_two, scale2)
     lanes_sent(0)
     lax.fori_loop(0, 32, lanes_back, 0)
     lanes_go(1)
+    back_go(1)
+    pair_stage(1)
+    mix(y)
+    part_turn(0)
     back(z)
     lanes_turn(1, 0)
+    part_turn(1)
     lanes_turn(1, 1)
     pass_stage(1)
-    for w in range(2):
-        for d in range(2, 6):
-            part_copy(w, 0, d).wait_recv()
-        part = parts[w]
-
-        def add_four(i, _):
-            a, b = i // 3, i % 3
-            here = (y, a) if w == 0 else (a, z)
-            total = part[here[0], here[1], b].astype(F32)
-            for d in range(2):
-                total = total + f_buf[w, d, a, b].astype(F32)
-            part[here[0], here[1], b] = total.astype(BF)
-            return 0
-
-        lax.fori_loop(0, 12, add_four, 0)
-        for d in range(1, 4):
-            part_copy(w, 1, d).start()
     for w, out in ((0, mixed), (1, dxo)):
         for d in range(1, 4):
             part_copy(w, 1, d).wait_recv()

time: 152 us -> 151 us (level)
  no operation moved by 1% of the time
where the time goes in v7:
time: 151 us; the launch traced here: 150 us
  Pallas kernels  150 us (99%)
    pallas_call x1, Pallas kernels, local(): pl.pallas_call(layer_kernel, out_shape=outs, in_specs=[ANY] * 4 + [SM] *...  141 us
    pallas_call x1, Pallas kernels, local(): pl.pallas_call(table_kernel, out_shape=[jax.ShapeDtypeStruct((256,), jnp....  5.8 us

profile of v7, /device:TPU:0, one launch (start us, length us, event | category | flops | bytes accessed | tf_op | source)
XLA Modules:
  0.0 150.2 jit_solution(1352141550406291787)
XLA Ops:
  0.6 5.8 %shard_map.120 = (s32[256]{0:T(256)}, s32[24,48]{1,0:T(8,128)}) custom-call(s32[192]{0:T(256)} %owner.1, s32[15,192]{1,0:T(8,128)} %bitcast.6, s32[15,288]{1,0:T(8,128)} %bitcast.4), custom_call_target="tpu_custom_call" | custom-call | tf_op jit(solution)/shard_map/pallas_call | solution.py:698
  6.4 141.1 %shard_map.121 = (bf16[192,384]{1,0:T(8,128)(2,1)}, bf16[192,384]{1,0:T(8,128)(2,1)}, bf16[12,15,16,128]{3,2,1,0:T(8,128)(2,1)}, bf16[18,15,16,128]{3,2,1,0:T(8,128)(2,1)}) custom-call(bf16[192,384]{1,0:T(8,128)(2,1)} %tok_ref.1, bf16[192,384]{1,0:T(8,128)(2,1)} %cot_ref.1, bf16[12,15,16,128]{3,2,1,0:T(8,128)(2,1)} %w1_ref.1, ...), custom_call_target="tpu_custom_call" | custom-call | tf_op jit(solution)/shard_map/pallas_call | solution.py:708
  147.5 2.6 %shard_map.122 = (bf16[192,384]{1,0:T(8,128)(2,1)}, bf16[192,384]{1,0:T(8,128)(2,1)}, bf16[12,15,16,128]{3,2,1,0:T(8,128)(2,1)}, bf16[18,15,16,128]{3,2,1,0:T(8,128)(2,1)}) custom-call(bf16[192,384]{1,0:T(8,128)(2,1)} %get-tuple-element.12.refs_0_, bf16[192,384]{1,0:T(8,128)(2,1)} %get-tuple-element.13.refs_1_, ...), custom_call_target="tpu_custom_call" | custom-call | tf_op jit(solution)/shard_map/pallas_call | solution.py:766

commit v8 on v7

--- a/solution.py
+++ b/solution.py
@@ -495,11 +495,11 @@
 
     for i in (4, 7, 8, 9):
         weight_copy(1, i).wait_recv()
+    pair_stage(0)
+    pl.semaphore_signal(free_sem, inc=1, device_id=(sp, t), device_id_type=MESH)
     mix((y + 2) % 4)
     part_copy(0, 0, 0).start()
     part_copy(0, 0, 1).start()
-    pair_stage(0)
-    pl.semaphore_signal(free_sem, inc=1, device_id=(sp, t), device_id_type=MESH)
     def hidden(g, _):
         w2c = jnp.concatenate([w2all[:, g, k].reshape(128, 128) for k in range(NK)], axis=1)
         dys = jnp.concatenate([dyall[col(g, k)] for k in range(NK)], axis=1)

time: 151 us -> 150 us (level)
  no operation moved by 1% of the time
where the time goes in v8:
time: 150 us
  Pallas kernels  149 us (99%)
    pallas_call x1, Pallas kernels, local(): pl.pallas_call(layer_kernel, out_shape=outs, in_specs=[ANY] * 4 + [SM] *...  141 us
    pallas_call x1, Pallas kernels, local(): pl.pallas_call(table_kernel, out_shape=[jax.ShapeDtypeStruct((256,), jnp....  5.8 us

profile of v8, /device:TPU:0, one launch (start us, length us, event | category | flops | bytes accessed | tf_op | source)
XLA Modules:
  0.0 149.7 jit_solution(12973999912622888587)
XLA Ops:
  0.6 5.8 %shard_map.120 = (s32[256]{0:T(256)}, s32[24,48]{1,0:T(8,128)}) custom-call(s32[192]{0:T(256)} %owner.1, s32[15,192]{1,0:T(8,128)} %bitcast.6, s32[15,288]{1,0:T(8,128)} %bitcast.4), custom_call_target="tpu_custom_call" | custom-call | tf_op jit(solution)/shard_map/pallas_call | solution.py:698
  6.4 140.7 %shard_map.121 = (bf16[192,384]{1,0:T(8,128)(2,1)}, bf16[192,384]{1,0:T(8,128)(2,1)}, bf16[12,15,16,128]{3,2,1,0:T(8,128)(2,1)}, bf16[18,15,16,128]{3,2,1,0:T(8,128)(2,1)}) custom-call(bf16[192,384]{1,0:T(8,128)(2,1)} %tok_ref.1, bf16[192,384]{1,0:T(8,128)(2,1)} %cot_ref.1, bf16[12,15,16,128]{3,2,1,0:T(8,128)(2,1)} %w1_ref.1, ...), custom_call_target="tpu_custom_call" | custom-call | tf_op jit(solution)/shard_map/pallas_call | solution.py:708
  147.1 2.6 %shard_map.122 = (bf16[192,384]{1,0:T(8,128)(2,1)}, bf16[192,384]{1,0:T(8,128)(2,1)}, bf16[12,15,16,128]{3,2,1,0:T(8,128)(2,1)}, bf16[18,15,16,128]{3,2,1,0:T(8,128)(2,1)}) custom-call(bf16[192,384]{1,0:T(8,128)(2,1)} %get-tuple-element.12.refs_0_, bf16[192,384]{1,0:T(8,128)(2,1)} %get-tuple-element.13.refs_1_, ...), custom_call_target="tpu_custom_call" | custom-call | tf_op jit(solution)/shard_map/pallas_call | solution.py:766

commit v9 on v8

--- a/solution.py
+++ b/solution.py
@@ -273,6 +273,17 @@
             )
     for cp in loads:
         cp.start()
+    loads[1].wait()
+
+    def scale_one(g, _):
+        for k in range(NK):
+            w1all[p, g, k] = (w1in[g, k].astype(F32) * scale1(g, k)).astype(BF)
+        return 0
+
+    lax.fori_loop(0, NB, scale_one, 0)
+    pl.semaphore_wait(barrier, 9)
+    for i in range(5):
+        weight_copy(0, i).start()
     loads[0].wait()
 
     def lanes_out(i, _):
@@ -281,18 +292,7 @@
         return 0
 
     lax.fori_loop(0, 32, lanes_out, 0)
-    pl.semaphore_wait(barrier, 9)
     lanes_go(0)
-    loads[1].wait()
-
-    def scale_one(g, _):
-        for k in range(NK):
-            w1all[p, g, k] = (w1in[g, k].astype(F32) * scale1(g, k)).astype(BF)
-        return 0
-
-    lax.fori_loop(0, NB, scale_one, 0)
-    for i in range(5):
-        weight_copy(0, i).start()
     w1all[:, :, NK] = jnp.zeros((8, NB, 16, 128), BF)
     w2all[:, :, NK] = jnp.zeros((8, NB, 16, 128), BF)
     for cp in loads[2:]:

time: 150 us -> 151 us (level)
  no operation moved by 1% of the time
where the time goes in v9:
time: 151 us; the launch traced here: 150 us
  Pallas kernels  150 us (99%)
    pallas_call x1, Pallas kernels, local(): pl.pallas_call(layer_kernel, out_shape=outs, in_specs=[ANY] * 4 + [SM] *...  141 us
    pallas_call x1, Pallas kernels, local(): pl.pallas_call(table_kernel, out_shape=[jax.ShapeDtypeStruct((256,), jnp....  5.8 us

profile of v9, /device:TPU:0, one launch (start us, length us, event | category | flops | bytes accessed | tf_op | source)
XLA Modules:
  0.0 150.5 jit_solution(1408753008991186251)
XLA Ops:
  0.6 5.8 %shard_map.120 = (s32[256]{0:T(256)}, s32[24,48]{1,0:T(8,128)}) custom-call(s32[192]{0:T(256)} %owner.1, s32[15,192]{1,0:T(8,128)} %bitcast.6, s32[15,288]{1,0:T(8,128)} %bitcast.4), custom_call_target="tpu_custom_call" | custom-call | tf_op jit(solution)/shard_map/pallas_call | solution.py:698
  6.4 141.4 %shard_map.121 = (bf16[192,384]{1,0:T(8,128)(2,1)}, bf16[192,384]{1,0:T(8,128)(2,1)}, bf16[12,15,16,128]{3,2,1,0:T(8,128)(2,1)}, bf16[18,15,16,128]{3,2,1,0:T(8,128)(2,1)}) custom-call(bf16[192,384]{1,0:T(8,128)(2,1)} %tok_ref.1, bf16[192,384]{1,0:T(8,128)(2,1)} %cot_ref.1, bf16[12,15,16,128]{3,2,1,0:T(8,128)(2,1)} %w1_ref.1, ...), custom_call_target="tpu_custom_call" | custom-call | tf_op jit(solution)/shard_map/pallas_call | solution.py:708
  147.8 2.6 %shard_map.122 = (bf16[192,384]{1,0:T(8,128)(2,1)}, bf16[192,384]{1,0:T(8,128)(2,1)}, bf16[12,15,16,128]{3,2,1,0:T(8,128)(2,1)}, bf16[18,15,16,128]{3,2,1,0:T(8,128)(2,1)}) custom-call(bf16[192,384]{1,0:T(8,128)(2,1)} %get-tuple-element.12.refs_0_, bf16[192,384]{1,0:T(8,128)(2,1)} %get-tuple-element.13.refs_1_, ...), custom_call_target="tpu_custom_call" | custom-call | tf_op jit(solution)/shard_map/pallas_call | solution.py:766
